TPU v7x, 32 devices: a whole 2x2x4 slice. The times are simulated.
32 devices in a mesh: cfg: 2 (over x), work: 16 (over z, y, core).
Axes of the slice: x: 2, y: 2, z: 4, core: 2. Of those that a mesh axis runs over, the one named last changes fastest.
Arguments:
- sources: bfloat16 [32, 16384, 128], P('cfg', 'work'), parts along dimension 0, may hold values from -6 to 6
- perambs: bfloat16 [192, 16384], P('cfg', 'work'), parts along dimension 0, may hold values from -0.5 to 0.5
- source_ids: int32 [16], replicated, may hold values from 0 to 15
- peramb_ids: int32 [48, 3], replicated, may hold values from 0 to 95
- sink_counts: int32 [16], replicated, may hold values from 1 to 6, 48 in all
- weights: float32 [48], replicated, may hold values from -2 to 2, as said below
Outputs:
- sink_tensors: bfloat16 [32, 16384, 128], P(('cfg', 'work')), parts along dimension 0
There are 2 independent parts, one for each index of `cfg`. A program takes and returns all parts, laid end to end along the dimension named above; an argument that names none is the same for every part. Nothing has to cross between parts.
Inputs may be any that keep to these rules, and one draw needn't show every extreme that they name: `sink_counts`: diagrams are listed sink by sink in order; the counts add up to 48 and some sink has exactly 6 diagrams. `weights`: nonzero multiples of 1/4.
All inputs are finite; a program needn't handle non-finite values.
Results may differ from a plain program's by a relative error of at most 0.0064.
Values may be sent and summed in bfloat16 or wider, within the bound.
No kernel may reach another device: no remote copies, remote signals or barrier semaphores. Data moves between devices by JAX's collectives and lax.ppermute only.
A program may use at most 128 MiB of HBM per device.

v0:
```python
import functools

import jax
import jax.numpy as jnp
from jax import lax
from jax.experimental import pallas as pl
from jax.experimental.pallas import tpu as pltpu
from jax.sharding import PartitionSpec as P

MOST = 6
LEGS = 3
UNIT_ROWS = 16
B_BLOCK = 64
ACC = jnp.bfloat16
GROUPS = ((0, 2, 4), (3, 5), (1, 6), (7,))
IN_FLIGHT = 5
FAR_TURNS = (2, 4, 5, 6, 10, 11)
HELD_BACK = 5
SMALL_VMEM = 16 * 1024 * 1024
ROOM = 13 * 1024 * 1024


def pieces_kernel(shifts, ids_ref, source_ref, *refs):
    piece_refs, (held_ref, in_sems, out_sems) = refs[: len(shifts)], refs[len(shifts) :]
    own = lax.axis_index("work")
    reads, writes = [], []
    for i, shift in enumerate(shifts):
        reads.append(
            pltpu.make_async_copy(
                source_ref.at[ids_ref[own ^ shift]], held_ref.at[i], in_sems.at[i]
            )
        )
        writes.append(pltpu.make_async_copy(held_ref.at[i], piece_refs[i], out_sems.at[i]))
        reads[i].start()
    for read, write in zip(reads, writes):
        read.wait()
        write.start()
    for write in writes:
        write.wait()


def choose_pieces(sources, source_ids, shifts):
    return pl.pallas_call(
        functools.partial(pieces_kernel, shifts),
        in_specs=[pl.BlockSpec(memory_space=pltpu.SMEM), pl.BlockSpec(memory_space=pl.ANY)],
        out_specs=[pl.BlockSpec(memory_space=pl.ANY)] * len(shifts),
        out_shape=[jax.ShapeDtypeStruct(sources.shape[1:], sources.dtype)] * len(shifts),
        scratch_shapes=[
            pltpu.VMEM((len(shifts), *sources.shape[1:]), sources.dtype),
            pltpu.SemaphoreType.DMA((len(shifts),)),
            pltpu.SemaphoreType.DMA((len(shifts),)),
        ],
        compiler_params=pltpu.CompilerParams(vmem_limit_bytes=SMALL_VMEM),
    )(source_ids, sources)


def matrices_kernel(workers, counts_ref, matrix_ids_ref, peramb_ref, matrix_ref, choice_ref, spread_ref):
    rows = MOST * LEGS
    diagrams = matrix_ids_ref.shape[1]
    total = peramb_ref.shape[0]
    lanes = lax.broadcasted_iota(jnp.int32, (1, total), 1)

    def mark(sink, start):
        for slot in range(MOST):
            diagram = jnp.minimum(start + slot, diagrams - 1)
            for leg in range(LEGS):
                choice_ref[pl.ds(sink * rows + slot * LEGS + leg, 1), :] = jnp.where(
                    lanes == matrix_ids_ref[leg, diagram], 1.0, 0.0
                )
        return start + counts_ref[sink]

    lax.fori_loop(0, workers, mark, 0)
    chosen = jnp.dot(
        choice_ref[...].astype(jnp.bfloat16), peramb_ref[...], preferred_element_type=jnp.float32
    )
    extent = matrix_ref.shape[2]
    a_per = peramb_ref.shape[1] // extent
    for row in range(a_per):
        spread_ref[pl.ds(row, workers * rows, stride=a_per), :] = chosen[
            :, row * extent : (row + 1) * extent
        ]
    matrix_ref[...] = spread_ref[...].reshape(matrix_ref.shape).astype(jnp.bfloat16)


def choose_matrices(perambs, peramb_ids, sink_counts, workers, extent):
    rows = MOST * LEGS
    a_per = perambs.shape[1] // extent
    smem = pl.BlockSpec(memory_space=pltpu.SMEM)
    vmem = pl.BlockSpec(memory_space=pltpu.VMEM)
    return pl.pallas_call(
        functools.partial(matrices_kernel, workers),
        in_specs=[smem, smem, vmem],
        out_specs=vmem,
        out_shape=jax.ShapeDtypeStruct((workers, rows * a_per, extent), jnp.bfloat16),
        scratch_shapes=[
            pltpu.VMEM((workers * rows, perambs.shape[0]), jnp.float32),
            pltpu.VMEM((workers * rows * a_per, extent), jnp.float32),
        ],
        compiler_params=pltpu.CompilerParams(vmem_limit_bytes=SMALL_VMEM),
    )(sink_counts, peramb_ids.T, perambs)


def legs_kernel(
    workers, counts_ref, weights_ref, matrix_ref, leg3_ref, leg2_ref, leg1_ref, flat_ref, leg_ref
):
    extent = matrix_ref.shape[2]
    rows = MOST * LEGS
    a_per = matrix_ref.shape[1] // rows
    flat_ref[...] = matrix_ref[...].astype(jnp.float32).reshape(flat_ref.shape)
    own = lax.axis_index("work")
    start = lax.fori_loop(0, own, lambda i, total: total + counts_ref[i], 0)
    count = counts_ref[own]
    unit = UNIT_ROWS // a_per
    units = workers // unit
    for slot in range(MOST):
        for leg in range(LEGS):
            base = (slot * LEGS + leg) * a_per
            for row in range(a_per):
                leg_ref[pl.ds(row, workers, stride=a_per), :] = flat_ref[
                    pl.ds(base + row, workers, stride=rows * a_per), :
                ]
            if leg == 2:
                leg3_ref[:, slot * extent : (slot + 1) * extent] = leg_ref[...].T.astype(
                    jnp.bfloat16
                )
            elif leg == 1:
                leg2_ref[slot * extent : (slot + 1) * extent, :] = leg_ref[...].astype(
                    jnp.bfloat16
                )
            else:
                diagram = jnp.minimum(start + slot, weights_ref.shape[0] - 1)
                factor = jnp.where(slot < count, weights_ref[diagram], 0.0)
                leg_ref[...] = (factor * leg_ref[...]).T
                for block in range(units):
                    place = (own // unit) ^ block
                    leg1_ref[block, slot * UNIT_ROWS : (slot + 1) * UNIT_ROWS, :] = leg_ref[
                        pl.ds(pl.multiple_of(place * UNIT_ROWS, UNIT_ROWS), UNIT_ROWS), :
                    ].astype(jnp.bfloat16)


def make_legs(matrices, sink_counts, weights, workers):
    extent = matrices.shape[2]
    a_per = extent // workers
    smem = pl.BlockSpec(memory_space=pltpu.SMEM)
    vmem = pl.BlockSpec(memory_space=pltpu.VMEM)
    return pl.pallas_call(
        functools.partial(legs_kernel, workers),
        in_specs=[smem, smem, vmem],
        out_specs=[vmem] * 3,
        out_shape=[
            jax.ShapeDtypeStruct((extent, MOST * extent), jnp.bfloat16),
            jax.ShapeDtypeStruct((MOST * extent, extent), jnp.bfloat16),
            jax.ShapeDtypeStruct(
                (extent // UNIT_ROWS, MOST * UNIT_ROWS, extent), jnp.bfloat16
            ),
        ],
        scratch_shapes=[
            pltpu.VMEM((matrices.shape[0] * matrices.shape[1], extent), jnp.float32),
            pltpu.VMEM((extent, extent), jnp.float32),
        ],
        compiler_params=pltpu.CompilerParams(vmem_limit_bytes=SMALL_VMEM),
    )(sink_counts, weights, matrices)


def group_kernel(first, last, units, per_unit, extent, *refs):
    pieces = len(units) * per_unit
    piece_refs = refs[:pieces]
    leg3_ref, leg2_ref, leg1_ref = refs[pieces : pieces + 3]
    refs = refs[pieces + 3 :]
    if not first:
        acc_ref, refs = refs[0], refs[1:]
    out_ref, turned_ref, outer_ref, across_ref, held_ref, sems = refs[:6]
    a_per = piece_refs[0].shape[0] // extent
    unit_depth = MOST * UNIT_ROWS
    depth = unit_depth * len(units)
    pitch = depth + 8
    step = pl.program_id(0)

    def fetch(piece):
        return pltpu.make_async_copy(piece_refs[piece], held_ref.at[piece], sems.at[piece])

    @pl.when(step == 0)
    def fetch_all():
        for piece in range(pieces):
            if not first:
                fetch(piece).start()

    def inner_legs(piece):
        place, lane = piece // per_unit, piece % per_unit
        if not first:
            fetch(piece).wait()
        rows_ref = piece_refs[piece] if first else held_ref.at[piece]
        sender = (lax.axis_index("work") & (per_unit - 1)) ^ lane
        third = jnp.dot(
            rows_ref[...], leg3_ref[...], preferred_element_type=jnp.float32
        ).astype(jnp.bfloat16)
        for d in range(MOST):
            columns = third[:, d * extent : (d + 1) * extent]
            wide = jnp.concatenate(
                [columns[a * extent : (a + 1) * extent] for a in range(a_per)], axis=1
            )
            second = jnp.dot(
                leg2_ref[d * extent : (d + 1) * extent, :],
                wide,
                preferred_element_type=jnp.float32,
            )
            for a in range(a_per):
                row = place * unit_depth + d * UNIT_ROWS + sender * a_per + a
                turned_ref[pl.ds(row, extent, stride=pitch), :] = second[
                    :, a * extent : (a + 1) * extent
                ]

    @pl.when(step == 0)
    def turn_outer():
        for place, unit in enumerate(units):
            outer_ref[place * unit_depth : (place + 1) * unit_depth, :] = leg1_ref[
                unit
            ].astype(jnp.float32)
        across_ref[...] = outer_ref[...].T.astype(jnp.bfloat16)

    for piece in range(pieces):
        pl.when(step == piece)(functools.partial(inner_legs, piece))

    @pl.when(step >= pieces)
    def outer_leg():
        begin = (step - pieces) * B_BLOCK
        wide = jnp.concatenate(
            [
                turned_ref[pl.ds(pl.multiple_of((begin + b) * pitch, 8), depth), :].astype(
                    jnp.bfloat16
                )
                for b in range(B_BLOCK)
            ],
            axis=1,
        )
        whole = jnp.dot(across_ref[...], wide, preferred_element_type=jnp.float32)
        for b in range(B_BLOCK):
            part = whole[:, b * extent : (b + 1) * extent]
            if not first:
                part = part + acc_ref[b].astype(jnp.float32)
            if last:
                refs[6][pl.ds(b, extent, stride=B_BLOCK + 8), :] = part
            else:
                out_ref[b] = part.astype(out_ref.dtype)
        if last:
            for a in range(extent):
                out_ref[a] = refs[6][pl.ds(a * (B_BLOCK + 8), B_BLOCK), :].astype(jnp.bfloat16)


def add_group(units, pieces, leg3, leg2, leg1, acc, last):
    extent = leg3.shape[0]
    count = len(pieces)
    per_unit = count // len(units)
    depth = MOST * UNIT_ROWS * len(units)
    first = acc is None
    blocks = extent // B_BLOCK

    def whole_spec(x):
        return pl.BlockSpec(x.shape, lambda i: (0,) * x.ndim)

    def block_of(i):
        return jnp.maximum(i - count, 0)

    operands = [*pieces, leg3, leg2, leg1]
    in_specs = [whole_spec(x) for x in operands]
    if not first:
        in_specs[:count] = [pl.BlockSpec(memory_space=pl.ANY)] * count
    if not first:
        operands.append(acc)
        in_specs.append(pl.BlockSpec((B_BLOCK, extent, extent), lambda i: (block_of(i), 0, 0)))
    scratch = [
        pltpu.VMEM((extent * (depth + 8), extent), jnp.float32),
        pltpu.VMEM((depth, extent), jnp.float32),
        pltpu.VMEM((extent, depth), jnp.bfloat16),
        pltpu.VMEM((count, *pieces[0].shape), jnp.bfloat16),
        pltpu.SemaphoreType.DMA((count,)),
    ]
    if last:
        out_shape = jax.ShapeDtypeStruct((extent, extent, extent), jnp.bfloat16)
        out_spec = pl.BlockSpec((extent, B_BLOCK, extent), lambda i: (0, block_of(i), 0))
        scratch.append(pltpu.VMEM((extent * (B_BLOCK + 8), extent), jnp.float32))
    else:
        out_shape = jax.ShapeDtypeStruct((extent, extent, extent), ACC)
        out_spec = pl.BlockSpec((B_BLOCK, extent, extent), lambda i: (block_of(i), 0, 0))
    rows = count * pieces[0].shape[0]
    return pl.pallas_call(
        functools.partial(group_kernel, first, last, units, per_unit, extent),
        grid=(count + blocks,),
        in_specs=in_specs,
        out_specs=out_spec,
        out_shape=out_shape,
        scratch_shapes=scratch,
        compiler_params=pltpu.CompilerParams(
            dimension_semantics=("arbitrary",), vmem_limit_bytes=ROOM + 4 * extent * extent * (depth + 8)
        ),
        cost_estimate=pl.CostEstimate(
            flops=6 * MOST * rows * extent * extent,
            bytes_accessed=12 * extent**3,
            transcendentals=0,
        ),
    )(*operands)


def per_device(sources, perambs, source_ids, peramb_ids, sink_counts, weights):
    workers = lax.axis_size("work")
    extent = sources.shape[2]
    per_unit = UNIT_ROWS * workers // extent
    half = workers // 2
    far = list(range(half, workers))
    upper, lower = list(range(half // 2, half)), list(range(2, half // 2))
    near = [1, *upper, *lower]
    order = []
    while far or near:
        take_far = far and (not near or len(order) in FAR_TURNS)
        order.append(far.pop(0) if take_far else near.pop(0))
    early, late = tuple(order[:IN_FLIGHT]), (0, *order[IN_FLIGHT:])
    pieces = dict(zip(early, choose_pieces(sources, source_ids, early)))
    pieces.update(zip(late, choose_pieces(sources, source_ids, late)))
    arrived = {0: pieces[0]}

    def send(place):
        shift = order[place]
        piece = pieces[shift]
        if place >= IN_FLIGHT:
            before = order[place - IN_FLIGHT]
            piece, arrived[before] = lax.optimization_barrier((piece, arrived[before]))
        arrived[shift] = lax.ppermute(piece, "work", [(i, i ^ shift) for i in range(workers)])

    for place in range(IN_FLIGHT):
        send(place)
    matrices = choose_matrices(perambs, peramb_ids, sink_counts, workers, extent)
    matrices = lax.all_to_all(matrices, "work", split_axis=0, concat_axis=0, tiled=True)
    leg3, leg2, leg1 = make_legs(matrices, sink_counts, weights, workers)
    for place in range(IN_FLIGHT, len(order) - HELD_BACK):
        send(place)

    acc = None
    for group, units in enumerate(GROUPS):
        members = [arrived[u * per_unit + lane] for u in units for lane in range(per_unit)]
        acc = add_group(units, members, leg3, leg2, leg1, acc, group == len(GROUPS) - 1)
        if group == 0:
            for place in range(len(order) - HELD_BACK, len(order)):
                shift = order[place]
                pieces[shift], acc = lax.optimization_barrier((pieces[shift], acc))
                send(place)
    return acc.reshape(1, extent * extent, extent)


def solution(mesh):
    return jax.shard_map(
        per_device,
        mesh=mesh,
        in_specs=(P("cfg", "work", None), P("cfg", "work"), P(), P(), P(), P()),
        out_specs=P(("cfg", "work"), None, None),
        check_vma=False,
    )
```

profile of v0, /device:TPU:11, one launch (start us, length us, event | category | flops | bytes accessed | tf_op | source)
XLA Modules:
  0.0 131.3 jit_solution(10167062319351412590)
XLA Ops:
  0.0 0.9 copy-done.1
  2.3 2.2 %shard_map.66 = bf16[16,144,128]{2,1,0:T(8,128)(2,1)} custom-call(s32[16]{0:T(128)S(1)} %copy-done.4, s32[3,48]{1,0:T(4,128)S(1)} %bitcast.2, bf16[96,1024]{1,0:T(8,128)(2,1)S(1)} %copy-done.1), custom_call_target="tpu_custom_call" | custom-call | tf_op jit(solution)/shard_map/pallas_call | solution.py:90
  4.5 6.6 %all-to-all-start = ((bf16[16,144,128]{2,1,0:T(8,128)(2,1)}), bf16[16,144,128]{2,1,0:T(8,128)(2,1)S(1)}, u32[]{:S(2)}, u32[]{:S(2)}) async-start(bf16[16,144,128]{2,1,0:T(8,128)(2,1)} %shard_map.66), calls=%async_computation | async-start | bytes 1179648 | tf_op jit(solution)/shard_map/all_to_all | solution.py:332
  11.1 2.2 %copy-done = bf16[16,1024,128]{2,1,0:T(8,128)(2,1)S(1)} copy-done((bf16[16,1024,128]{2,1,0:T(8,128)(2,1)S(1)}, bf16[16,1024,128]{2,1,0:T(8,128)(2,1)}, u32[]{:S(2)}) %copy-start) | copy-done | bytes 4194328
  13.9 0.9 shard_map.65
  15.2 1.8 %collective-permute-start.2 = (bf16[1024,128]{1,0:T(8,128)(2,1)S(1)}, bf16[1024,128]{1,0:T(8,128)(2,1)S(1)}, u32[]{:S(2)}, u32[]{:S(2)}) collective-permute-start(bf16[1024,128]{1,0:T(8,128)(2,1)S(1)} %get-tuple-element.66), channel_id=1, source_target_pairs={{0,5},{1,4},{2,7},{3,6},{4,1},{5,0},{6,3},{7,2},{8,13},{9,12},{10,... | collective-permute-start | bytes 786440 | tf_op jit(solution)/shard_map/ppermute | solution.py:327
  17.0 2.1 %collective-permute-start.3 = (bf16[1024,128]{1,0:T(8,128)(2,1)S(1)}, bf16[1024,128]{1,0:T(8,128)(2,1)S(1)}, u32[]{:S(2)}, u32[]{:S(2)}) collective-permute-start(bf16[1024,128]{1,0:T(8,128)(2,1)S(1)} %get-tuple-element.69), channel_id=1, source_target_pairs={{0,8},{1,9},{2,10},{3,11},{4,12},{5,13},{6,14},{7,15},{8,0},{9,1},... | collective-permute-start | bytes 786440 | tf_op jit(solution)/shard_map/ppermute | solution.py:327
  19.6 2.0 %shard_map.64 = (bf16[1024,128]{1,0:T(8,128)(2,1)S(1)}, bf16[1024,128]{1,0:T(8,128)(2,1)}, bf16[1024,128]{1,0:T(8,128)(2,1)}, bf16[1024,128]{1,0:T(8,128)(2,1)},...) custom-call(s32[16]{0:T(128)S(1)} %copy-done.3, ...), custom_call_target="tpu_custom_call" | custom-call | tf_op jit(solution)/shard_map/pallas_call | solution.py:43
  23.0 12.4 %collective-permute-done.1.refs_2_ = bf16[1024,128]{1,0:T(8,128)(2,1)S(1)} collective-permute-done((bf16[1024,128]{1,0:T(8,128)(2,1)S(1)}, bf16[1024,128]{1,0:T(8,128)(2,1)S(1)}, u32[]{:S(2)}, u32[]{:S(2)}) %collective-permute-start.1) | collective-permute-done | bytes 262176 | tf_op jit(solution)/shard_map/ppermute | solution.py:327
  36.1 5.1 %collective-permute-done.2.refs_3_ = bf16[1024,128]{1,0:T(8,128)(2,1)S(1)} collective-permute-done((bf16[1024,128]{1,0:T(8,128)(2,1)S(1)}, bf16[1024,128]{1,0:T(8,128)(2,1)S(1)}, u32[]{:S(2)}, u32[]{:S(2)}) %collective-permute-start.2) | collective-permute-done | bytes 262176 | tf_op jit(solution)/shard_map/ppermute | solution.py:327
  42.6 4.0 %collective-permute-done.4.refs_5_ = bf16[1024,128]{1,0:T(8,128)(2,1)S(1)} collective-permute-done((bf16[1024,128]{1,0:T(8,128)(2,1)S(1)}, bf16[1024,128]{1,0:T(8,128)(2,1)S(1)}, u32[]{:S(2)}, u32[]{:S(2)}) %collective-permute-start.4) | collective-permute-done | bytes 262176 | tf_op jit(solution)/shard_map/ppermute | solution.py:327
  47.3 4.3 %collective-permute-start.5 = (bf16[1024,128]{1,0:T(8,128)(2,1)}, bf16[1024,128]{1,0:T(8,128)(2,1)S(1)}, u32[]{:S(2)}, u32[]{:S(2)}) collective-permute-start(bf16[1024,128]{1,0:T(8,128)(2,1)} %get-tuple-element.81), channel_id=1, source_target_pairs={{0,7},{1,6},{2,5},{3,4},{4,3},{5,2},{6,1},{7,0},{8,15},{9,14},{10,... | collective-permute-start | bytes 786440 | tf_op jit(solution)/shard_map/ppermute | solution.py:327
  51.8 2.4 %collective-permute-start.11 = (bf16[1024,128]{1,0:T(8,128)(2,1)}, bf16[1024,128]{1,0:T(8,128)(2,1)S(1)}, u32[]{:S(2)}, u32[]{:S(2)}) collective-permute-start(bf16[1024,128]{1,0:T(8,128)(2,1)} %get-tuple-element.93), channel_id=1, source_target_pairs={{0,10},{1,11},{2,8},{3,9},{4,14},{5,15},{6,12},{7,13},{8,2},{9,3},... | collective-permute-start | bytes 786440 | tf_op jit(solution)/shard_map/ppermute | solution.py:327
  54.2 1.7 %collective-permute-start.13 = (bf16[1024,128]{1,0:T(8,128)(2,1)}, bf16[1024,128]{1,0:T(8,128)(2,1)S(1)}, u32[]{:S(2)}, u32[]{:S(2)}) collective-permute-start(bf16[1024,128]{1,0:T(8,128)(2,1)} %get-tuple-element.96), channel_id=1, source_target_pairs={{0,11},{1,10},{2,9},{3,8},{4,15},{5,14},{6,13},{7,12},{8,3},{9,2},... | collective-permute-start | bytes 786440 | tf_op jit(solution)/shard_map/ppermute | solution.py:327
  55.9 1.7 %shard_map.67 = (bf16[128,768]{1,0:T(8,128)(2,1)S(1)}, bf16[768,128]{1,0:T(8,128)(2,1)S(1)}, bf16[8,96,128]{2,1,0:T(8,128)(2,1)S(1)}) custom-call(s32[16]{0:T(128)S(1)} %copy-done.5, f32[48]{0:T(128)S(1)} %copy-done.6, bf16[16,144,128]{2,1,0:T(8,128)(2,1)S(1)} %all-to-all-done.matrix_ref), custom_call_target="tpu_custom_call" | custom-call | tf_op jit(solution)/shard_map/pallas_call | solution.py:146
  57.6 0.9 copy-done.8
  58.6 0.9 copy-done.10
  59.5 0.9 copy-done.12
  60.5 0.9 copy-done.14
  61.4 0.9 copy-done.16
  62.4 0.9 copy-done.18
  63.3 9.2 %shard_map.68.refs_7_ = bf16[128,128,128]{2,1,0:T(8,128)(2,1)S(1)} custom-call(bf16[1024,128]{1,0:T(8,128)(2,1)S(1)} %copy-done.18, bf16[1024,128]{1,0:T(8,128)(2,1)S(1)} %copy-done.8, bf16[1024,128]{1,0:T(8,128)(2,1)S(1)} %copy-done.10, bf16[1024,128]{1,0:T(8,128)(2,1)S(1)} %copy-done.12, bf16[1024,128]{1,0:T(8,128)(2,1)S(1)} %copy-done.14, ...), custom_call_target="tpu_custom_call" | custom-call | flops 3623878656 | bytes 25165824 | tf_op jit(solution)/shard_map/pallas_call | solution.py:286
  72.5 0.7 collective-permute-start.10
  73.3 1.1 collective-permute-start.12
  74.3 1.9 %collective-permute-done.13.refs_3_ = bf16[1024,128]{1,0:T(8,128)(2,1)S(1)} collective-permute-done((bf16[1024,128]{1,0:T(8,128)(2,1)}, bf16[1024,128]{1,0:T(8,128)(2,1)S(1)}, u32[]{:S(2)}, u32[]{:S(2)}) %collective-permute-start.13) | collective-permute-done | bytes 262176 | tf_op jit(solution)/shard_map/ppermute | solution.py:327
  76.2 9.7 %collective-permute-start.14 = (bf16[1024,128]{1,0:T(8,128)(2,1)S(1)}, bf16[1024,128]{1,0:T(8,128)(2,1)S(1)}, u32[]{:S(2)}, u32[]{:S(2)}) collective-permute-start(bf16[1024,128]{1,0:T(8,128)(2,1)S(1)} %get-tuple-element.97), channel_id=1, source_target_pairs={{0,13},{1,12},{2,15},{3,14},{4,9},{5,8},{6,11},{7,10},{8,5},{9,4},... | collective-permute-start | bytes 786440 | tf_op jit(solution)/shard_map/ppermute | solution.py:327
  85.9 1.1 collective-permute-start.6
  87.4 6.1 %shard_map.69.refs_7_ = bf16[128,128,128]{2,1,0:T(8,128)(2,1)S(1)} custom-call(bf16[1024,128]{1,0:T(8,128)(2,1)S(1)} %collective-permute-done.9.refs_0_, bf16[1024,128]{1,0:T(8,128)(2,1)S(1)} %collective-permute-done.5.refs_1_, bf16[1024,128]{1,0:T(8,128)(2,1)S(1)} %collective-permute-done.11.refs_2_, bf16[1024,128]{1,0:T(8,128)(2,1)S(1)} %collective-permute-done.13.refs_3_, ...), custom_call_target="tpu_custom_call" | custom-call | flops 2415919104 | bytes 25165824 | tf_op jit(solution)/shard_map/pallas_call | solution.py:286
  93.6 20.5 %collective-permute-done.14.refs_3_ = bf16[1024,128]{1,0:T(8,128)(2,1)S(1)} collective-permute-done((bf16[1024,128]{1,0:T(8,128)(2,1)S(1)}, bf16[1024,128]{1,0:T(8,128)(2,1)S(1)}, u32[]{:S(2)}, u32[]{:S(2)}) %collective-permute-start.14) | collective-permute-done | bytes 262176 | tf_op jit(solution)/shard_map/ppermute | solution.py:327
  114.1 6.1 %shard_map.70.refs_5_ = bf16[128,128,128]{2,1,0:T(8,128)(2,1)S(1)} custom-call(bf16[1024,128]{1,0:T(8,128)(2,1)S(1)} %collective-permute-done.7.refs_0_, bf16[1024,128]{1,0:T(8,128)(2,1)S(1)} %collective-permute-done.10.refs_1_, bf16[1024,128]{1,0:T(8,128)(2,1)S(1)} %collective-permute-done.12.refs_2_, ...), custom_call_target="tpu_custom_call" | custom-call | flops 2415919104 | bytes 25165824 | tf_op jit(solution)/shard_map/pallas_call | solution.py:286
  120.2 4.7 %collective-permute-done.8.refs_1_ = bf16[1024,128]{1,0:T(8,128)(2,1)S(1)} collective-permute-done((bf16[1024,128]{1,0:T(8,128)(2,1)S(1)}, bf16[1024,128]{1,0:T(8,128)(2,1)S(1)}, u32[]{:S(2)}, u32[]{:S(2)}) %collective-permute-start.8) | collective-permute-done | bytes 262176 | tf_op jit(solution)/shard_map/ppermute | solution.py:327
  124.9 6.2 %shard_map.71 = bf16[128,128,128]{2,1,0:T(8,128)(2,1)} custom-call(bf16[1024,128]{1,0:T(8,128)(2,1)S(1)} %collective-permute-done.6.refs_0_, bf16[1024,128]{1,0:T(8,128)(2,1)S(1)} %collective-permute-done.8.refs_1_, bf16[128,768]{1,0:T(8,128)(2,1)S(1)} %get-tuple-element.74.refs_6_.refs_4_.refs_2_, ...), custom_call_target="tpu_custom_call" | custom-call | flops 1207959552 | bytes 25165824 | tf_op jit(solution)/shard_map/pallas_call | solution.py:286
  (46 shorter events, 7.8 us)
Async XLA Ops:
  0.0 0.9 copy-start.1
  4.5 51.4 %all-to-all-start = ((bf16[16,144,128]{2,1,0:T(8,128)(2,1)}), bf16[16,144,128]{2,1,0:T(8,128)(2,1)S(1)}, u32[]{:S(2)}, u32[]{:S(2)}) async-start(bf16[16,144,128]{2,1,0:T(8,128)(2,1)} %shard_map.66), calls=%async_computation | async-start | bytes 1179648 | tf_op jit(solution)/shard_map/all_to_all | solution.py:332
  11.1 2.2 %copy-start = (bf16[16,1024,128]{2,1,0:T(8,128)(2,1)S(1)}, bf16[16,1024,128]{2,1,0:T(8,128)(2,1)}, u32[]{:S(2)}) copy-start(bf16[16,1024,128]{2,1,0:T(8,128)(2,1)} %source_ref.3) | copy-start | bytes 12582916
  13.9 42.0 %copy-start.5 = (s32[16]{0:T(128)S(1)}, s32[16]{0:T(128)}, u32[]{:S(2)}) copy-start(s32[16]{0:T(128)} %counts_ref.3) | copy-start | bytes 196
  13.9 42.0 %copy-start.6 = (f32[48]{0:T(128)S(1)}, f32[48]{0:T(128)}, u32[]{:S(2)}) copy-start(f32[48]{0:T(128)} %weights_ref.1) | copy-start | bytes 580
  14.8 7.5 %collective-permute-start = (bf16[1024,128]{1,0:T(8,128)(2,1)S(1)}, bf16[1024,128]{1,0:T(8,128)(2,1)S(1)}, u32[]{:S(2)}, u32[]{:S(2)}) collective-permute-start(bf16[1024,128]{1,0:T(8,128)(2,1)S(1)} %get-tuple-element.60), channel_id=1, source_target_pairs={{0,1},{1,0},{2,3},{3,2},{4,5},{5,4},{6,7},{7,6},{8,9},{9,8},{10,11... | collective-permute-start | bytes 786440 | tf_op jit(solution)/shard_map/ppermute | solution.py:327
  15.2 20.2 %collective-permute-start.1 = (bf16[1024,128]{1,0:T(8,128)(2,1)S(1)}, bf16[1024,128]{1,0:T(8,128)(2,1)S(1)}, u32[]{:S(2)}, u32[]{:S(2)}) collective-permute-start(bf16[1024,128]{1,0:T(8,128)(2,1)S(1)} %get-tuple-element.63), channel_id=1, source_target_pairs={{0,4},{1,5},{2,6},{3,7},{4,0},{5,1},{6,2},{7,3},{8,12},{9,13},{10,... | collective-permute-start | bytes 786440 | tf_op jit(solution)/shard_map/ppermute | solution.py:327
  15.2 25.9 %collective-permute-start.2 = (bf16[1024,128]{1,0:T(8,128)(2,1)S(1)}, bf16[1024,128]{1,0:T(8,128)(2,1)S(1)}, u32[]{:S(2)}, u32[]{:S(2)}) collective-permute-start(bf16[1024,128]{1,0:T(8,128)(2,1)S(1)} %get-tuple-element.66), channel_id=1, source_target_pairs={{0,5},{1,4},{2,7},{3,6},{4,1},{5,0},{6,3},{7,2},{8,13},{9,12},{10,... | collective-permute-start | bytes 786440 | tf_op jit(solution)/shard_map/ppermute | solution.py:327
  17.0 24.8 %collective-permute-start.3 = (bf16[1024,128]{1,0:T(8,128)(2,1)S(1)}, bf16[1024,128]{1,0:T(8,128)(2,1)S(1)}, u32[]{:S(2)}, u32[]{:S(2)}) collective-permute-start(bf16[1024,128]{1,0:T(8,128)(2,1)S(1)} %get-tuple-element.69), channel_id=1, source_target_pairs={{0,8},{1,9},{2,10},{3,11},{4,12},{5,13},{6,14},{7,15},{8,0},{9,1},... | collective-permute-start | bytes 786440 | tf_op jit(solution)/shard_map/ppermute | solution.py:327
  19.1 27.4 %collective-permute-start.4 = (bf16[1024,128]{1,0:T(8,128)(2,1)S(1)}, bf16[1024,128]{1,0:T(8,128)(2,1)S(1)}, u32[]{:S(2)}, u32[]{:S(2)}) collective-permute-start(bf16[1024,128]{1,0:T(8,128)(2,1)S(1)} %get-tuple-element.72), channel_id=1, source_target_pairs={{0,9},{1,8},{2,11},{3,10},{4,13},{5,12},{6,15},{7,14},{8,1},{9,0},... | collective-permute-start | bytes 786440 | tf_op jit(solution)/shard_map/ppermute | solution.py:327
  21.6 0.7 copy-start.17
  22.3 0.7 copy-start.7
  35.4 0.7 copy-start.9
  41.2 0.7 copy-start.11
  41.9 0.7 copy-start.13
  46.6 0.7 copy-start.15
  47.3 38.6 %collective-permute-start.5 = (bf16[1024,128]{1,0:T(8,128)(2,1)}, bf16[1024,128]{1,0:T(8,128)(2,1)S(1)}, u32[]{:S(2)}, u32[]{:S(2)}) collective-permute-start(bf16[1024,128]{1,0:T(8,128)(2,1)} %get-tuple-element.81), channel_id=1, source_target_pairs={{0,7},{1,6},{2,5},{3,4},{4,3},{5,2},{6,1},{7,0},{8,15},{9,14},{10,... | collective-permute-start | bytes 786440 | tf_op jit(solution)/shard_map/ppermute | solution.py:327
  51.6 35.4 %collective-permute-start.7 = (bf16[1024,128]{1,0:T(8,128)(2,1)S(1)}, bf16[1024,128]{1,0:T(8,128)(2,1)S(1)}, u32[]{:S(2)}, u32[]{:S(2)}) collective-permute-start(bf16[1024,128]{1,0:T(8,128)(2,1)S(1)} %get-tuple-element.86), channel_id=1, source_target_pairs={{0,2},{1,3},{2,0},{3,1},{4,6},{5,7},{6,4},{7,5},{8,10},{9,11},{10,... | collective-permute-start | bytes 786440 | tf_op jit(solution)/shard_map/ppermute | solution.py:327
  51.8 20.7 %collective-permute-start.9 = (bf16[1024,128]{1,0:T(8,128)(2,1)}, bf16[1024,128]{1,0:T(8,128)(2,1)S(1)}, u32[]{:S(2)}, u32[]{:S(2)}) collective-permute-start(bf16[1024,128]{1,0:T(8,128)(2,1)} %get-tuple-element.90), channel_id=1, source_target_pairs={{0,6},{1,7},{2,4},{3,5},{4,2},{5,3},{6,0},{7,1},{8,14},{9,15},{10,... | collective-permute-start | bytes 786440 | tf_op jit(solution)/shard_map/ppermute | solution.py:327
  51.8 21.4 %collective-permute-start.11 = (bf16[1024,128]{1,0:T(8,128)(2,1)}, bf16[1024,128]{1,0:T(8,128)(2,1)S(1)}, u32[]{:S(2)}, u32[]{:S(2)}) collective-permute-start(bf16[1024,128]{1,0:T(8,128)(2,1)} %get-tuple-element.93), channel_id=1, source_target_pairs={{0,10},{1,11},{2,8},{3,9},{4,14},{5,15},{6,12},{7,13},{8,2},{9,3},... | collective-permute-start | bytes 786440 | tf_op jit(solution)/shard_map/ppermute | solution.py:327
  54.2 22.0 %collective-permute-start.13 = (bf16[1024,128]{1,0:T(8,128)(2,1)}, bf16[1024,128]{1,0:T(8,128)(2,1)S(1)}, u32[]{:S(2)}, u32[]{:S(2)}) collective-permute-start(bf16[1024,128]{1,0:T(8,128)(2,1)} %get-tuple-element.96), channel_id=1, source_target_pairs={{0,11},{1,10},{2,9},{3,8},{4,15},{5,14},{6,13},{7,12},{8,3},{9,2},... | collective-permute-start | bytes 786440 | tf_op jit(solution)/shard_map/ppermute | solution.py:327
  57.6 1.0 copy-start.8
  58.6 0.9 copy-start.10
  59.5 0.9 copy-start.12
  60.5 0.9 copy-start.14
  61.4 0.9 copy-start.16
  62.4 0.9 copy-start.18
  72.5 21.0 %collective-permute-start.10 = (bf16[1024,128]{1,0:T(8,128)(2,1)S(1)}, bf16[1024,128]{1,0:T(8,128)(2,1)S(1)}, u32[]{:S(2)}, u32[]{:S(2)}) collective-permute-start(bf16[1024,128]{1,0:T(8,128)(2,1)S(1)} %get-tuple-element.91), channel_id=1, source_target_pairs={{0,3},{1,2},{2,1},{3,0},{4,7},{5,6},{6,5},{7,4},{8,11},{9,10},{10,... | collective-permute-start | bytes 786440 | tf_op jit(solution)/shard_map/ppermute | solution.py:327
  73.3 20.3 %collective-permute-start.12 = (bf16[1024,128]{1,0:T(8,128)(2,1)S(1)}, bf16[1024,128]{1,0:T(8,128)(2,1)S(1)}, u32[]{:S(2)}, u32[]{:S(2)}) collective-permute-start(bf16[1024,128]{1,0:T(8,128)(2,1)S(1)} %get-tuple-element.94), channel_id=1, source_target_pairs={{0,12},{1,13},{2,14},{3,15},{4,8},{5,9},{6,10},{7,11},{8,4},{9,5},... | collective-permute-start | bytes 786440 | tf_op jit(solution)/shard_map/ppermute | solution.py:327
  76.2 37.8 %collective-permute-start.14 = (bf16[1024,128]{1,0:T(8,128)(2,1)S(1)}, bf16[1024,128]{1,0:T(8,128)(2,1)S(1)}, u32[]{:S(2)}, u32[]{:S(2)}) collective-permute-start(bf16[1024,128]{1,0:T(8,128)(2,1)S(1)} %get-tuple-element.97), channel_id=1, source_target_pairs={{0,13},{1,12},{2,15},{3,14},{4,9},{5,8},{6,11},{7,10},{8,5},{9,4},... | collective-permute-start | bytes 786440 | tf_op jit(solution)/shard_map/ppermute | solution.py:327
  85.9 34.3 %collective-permute-start.6 = (bf16[1024,128]{1,0:T(8,128)(2,1)S(1)}, bf16[1024,128]{1,0:T(8,128)(2,1)S(1)}, u32[]{:S(2)}, u32[]{:S(2)}) collective-permute-start(bf16[1024,128]{1,0:T(8,128)(2,1)S(1)} %get-tuple-element.82), channel_id=1, source_target_pairs={{0,14},{1,15},{2,12},{3,13},{4,10},{5,11},{6,8},{7,9},{8,6},{9,7},... | collective-permute-start | bytes 786440 | tf_op jit(solution)/shard_map/ppermute | solution.py:327
  87.0 37.9 %collective-permute-start.8 = (bf16[1024,128]{1,0:T(8,128)(2,1)S(1)}, bf16[1024,128]{1,0:T(8,128)(2,1)S(1)}, u32[]{:S(2)}, u32[]{:S(2)}) collective-permute-start(bf16[1024,128]{1,0:T(8,128)(2,1)S(1)} %get-tuple-element.87), channel_id=1, source_target_pairs={{0,15},{1,14},{2,13},{3,12},{4,11},{5,10},{6,9},{7,8},{8,7},{9,6},... | collective-permute-start | bytes 786440 | tf_op jit(solution)/shard_map/ppermute | solution.py:327
  (3 other events, 2.0 us)
where the time goes:
time: 132 us; the launch traced here: 131 us
  waiting for transfers between devices  48.5 us (37%)
  Pallas kernels  34.4 us (26%)
  starting transfers between devices  33 us (25%)
  local copies, waits for them, and re-layouts  15 us (11%)
    ppermute x15, waiting for transfers between devices, send(): lax.ppermute(piece, 'work', [(i, i ^ shift) for i in range(workers)])  48.5 us
    pallas_call x4, Pallas kernels, add_group(): pl.pallas_call(functools.partial(group_kernel, first, last, units, per_un...  27.7 us
    ppermute x15, starting transfers between devices, send(): lax.ppermute(piece, 'work', [(i, i ^ shift) for i in range(workers)])  26.4 us
    unnamed x38, local copies, waits for them, and re-layouts  15 us
    all_to_all x1, starting transfers between devices, per_device(): lax.all_to_all(matrices, 'work', split_axis=0, concat_axis=0, tiled=True)  6.61 us
    pallas_call x2, Pallas kernels, choose_pieces(): pl.pallas_call(functools.partial(pieces_kernel, shifts), in_specs=[pl.Blo...  2.84 us
  transfers between devices with their start and end apart: 16, of which 6 were waited for; matrix products, arithmetic and copies ran while one was open for 0% of the time, Pallas kernels for 20%

commit v1 on v0

--- a/solution.py
+++ b/solution.py
@@ -14,10 +14,10 @@
 ACC = jnp.bfloat16
 GROUPS = ((0, 2, 4), (3, 5), (1, 6), (7,))
 IN_FLIGHT = 5
-FAR_TURNS = (2, 4, 5, 6, 10, 11)
-HELD_BACK = 5
+FAR_TURNS = (2, 4)
 SMALL_VMEM = 16 * 1024 * 1024
 ROOM = 13 * 1024 * 1024
+FIRST_VMEM = 60 * 1024 * 1024
 
 
 def pieces_kernel(shifts, ids_ref, source_ref, *refs):
@@ -291,7 +291,7 @@
         out_shape=out_shape,
         scratch_shapes=scratch,
         compiler_params=pltpu.CompilerParams(
-            dimension_semantics=("arbitrary",), vmem_limit_bytes=ROOM + 4 * extent * extent * (depth + 8)
+            dimension_semantics=("arbitrary",), vmem_limit_bytes=FIRST_VMEM if first else ROOM + 4 * extent * extent * (depth + 8)
         ),
         cost_estimate=pl.CostEstimate(
             flops=6 * MOST * rows * extent * extent,
@@ -307,11 +307,11 @@
     per_unit = UNIT_ROWS * workers // extent
     half = workers // 2
     far = list(range(half, workers))
-    upper, lower = list(range(half // 2, half)), list(range(2, half // 2))
-    near = [1, *upper, *lower]
+    near = [s for pair in zip(range(half // 2), range(half // 2, half)) for s in pair][1:]
+    near = [1, *(s for s in near if s != 1)]
     order = []
     while far or near:
-        take_far = far and (not near or len(order) in FAR_TURNS)
+        take_far = far and (not near or len(order) % IN_FLIGHT in FAR_TURNS)
         order.append(far.pop(0) if take_far else near.pop(0))
     early, late = tuple(order[:IN_FLIGHT]), (0, *order[IN_FLIGHT:])
     pieces = dict(zip(early, choose_pieces(sources, source_ids, early)))
@@ -331,18 +331,13 @@
     matrices = choose_matrices(perambs, peramb_ids, sink_counts, workers, extent)
     matrices = lax.all_to_all(matrices, "work", split_axis=0, concat_axis=0, tiled=True)
     leg3, leg2, leg1 = make_legs(matrices, sink_counts, weights, workers)
-    for place in range(IN_FLIGHT, len(order) - HELD_BACK):
+    for place in range(IN_FLIGHT, len(order)):
         send(place)
 
     acc = None
     for group, units in enumerate(GROUPS):
         members = [arrived[u * per_unit + lane] for u in units for lane in range(per_unit)]
         acc = add_group(units, members, leg3, leg2, leg1, acc, group == len(GROUPS) - 1)
-        if group == 0:
-            for place in range(len(order) - HELD_BACK, len(order)):
-                shift = order[place]
-                pieces[shift], acc = lax.optimization_barrier((pieces[shift], acc))
-                send(place)
     return acc.reshape(1, extent * extent, extent)
 
 

time: 132 us -> 128 us (0.970)
  the two profiles are of different devices: /device:TPU:11 before, /device:TPU:0 now
where the time goes in v1:
time: 128 us
  waiting for transfers between devices  52.5 us (41%)
  Pallas kernels  37.9 us (30%)
  starting transfers between devices  27 us (21%)
  local copies, waits for them, and re-layouts  10 us (8%)
    ppermute x15, waiting for transfers between devices, send(): lax.ppermute(piece, 'work', [(i, i ^ shift) for i in range(workers)])  52.5 us
    pallas_call x4, Pallas kernels, add_group(): pl.pallas_call(functools.partial(group_kernel, first, last, units, per_un...  31.1 us
    ppermute x15, starting transfers between devices, send(): lax.ppermute(piece, 'work', [(i, i ^ shift) for i in range(workers)])  19.6 us
    unnamed x40, local copies, waits for them, and re-layouts  10 us
    all_to_all x1, starting transfers between devices, per_device(): lax.all_to_all(matrices, 'work', split_axis=0, concat_axis=0, tiled=True)  7.38 us
    pallas_call x2, Pallas kernels, choose_pieces(): pl.pallas_call(functools.partial(pieces_kernel, shifts), in_specs=[pl.Blo...  2.93 us
  transfers between devices with their start and end apart: 16, of which 4 were waited for; matrix products, arithmetic and copies ran while one was open for 0% of the time, Pallas kernels for 23%

profile of v1, /device:TPU:0, one launch (start us, length us, event | category | flops | bytes accessed | tf_op | source)
XLA Modules:
  0.0 127.7 jit_solution(9220626394183914358)
XLA Ops:
  0.0 0.9 copy-done.8
  0.9 0.7 copy-done.9
  1.6 0.7 copy-done.11
  2.3 2.2 %shard_map.66 = bf16[16,144,128]{2,1,0:T(8,128)(2,1)} custom-call(s32[16]{0:T(128)S(1)} %copy-done.11, s32[3,48]{1,0:T(4,128)S(1)} %bitcast.2, bf16[96,1024]{1,0:T(8,128)(2,1)S(1)} %copy-done.8), custom_call_target="tpu_custom_call" | custom-call | tf_op jit(solution)/shard_map/pallas_call | solution.py:90
  4.5 7.4 %all-to-all-start = ((bf16[16,144,128]{2,1,0:T(8,128)(2,1)}), bf16[16,144,128]{2,1,0:T(8,128)(2,1)S(1)}, u32[]{:S(2)}, u32[]{:S(2)}) async-start(bf16[16,144,128]{2,1,0:T(8,128)(2,1)} %shard_map.66), calls=%async_computation | async-start | bytes 1179648 | tf_op jit(solution)/shard_map/all_to_all | solution.py:332
  11.9 2.2 %copy-done = bf16[16,1024,128]{2,1,0:T(8,128)(2,1)S(1)} copy-done((bf16[16,1024,128]{2,1,0:T(8,128)(2,1)S(1)}, bf16[16,1024,128]{2,1,0:T(8,128)(2,1)}, u32[]{:S(2)}) %copy-start) | copy-done | bytes 4194328
  14.0 0.7 copy-done.10
  14.7 0.9 shard_map.65
  15.6 2.9 %collective-permute-start.11 = (bf16[1024,128]{1,0:T(8,128)(2,1)S(1)}, bf16[1024,128]{1,0:T(8,128)(2,1)S(1)}, u32[]{:S(2)}, u32[]{:S(2)}) collective-permute-start(bf16[1024,128]{1,0:T(8,128)(2,1)S(1)} %get-tuple-element.70), channel_id=1, source_target_pairs={{0,8},{1,9},{2,10},{3,11},{4,12},{5,13},{6,14},{7,15},{8,0},{9,1},... | collective-permute-start | bytes 786440 | tf_op jit(solution)/shard_map/ppermute | solution.py:327
  18.5 1.5 %collective-permute-start.8 = (bf16[1024,128]{1,0:T(8,128)(2,1)S(1)}, bf16[1024,128]{1,0:T(8,128)(2,1)S(1)}, u32[]{:S(2)}, u32[]{:S(2)}) collective-permute-start(bf16[1024,128]{1,0:T(8,128)(2,1)S(1)} %get-tuple-element.65), channel_id=1, source_target_pairs={{0,4},{1,5},{2,6},{3,7},{4,0},{5,1},{6,2},{7,3},{8,12},{9,13},{10,... | collective-permute-start | bytes 786440 | tf_op jit(solution)/shard_map/ppermute | solution.py:327
  19.9 0.7 collective-permute-start.3
  20.6 2.1 %shard_map.64 = (bf16[1024,128]{1,0:T(8,128)(2,1)S(1)}, bf16[1024,128]{1,0:T(8,128)(2,1)S(1)}, bf16[1024,128]{1,0:T(8,128)(2,1)S(1)}, bf16[1024,128]{1,0:T(8,128...) custom-call(s32[16]{0:T(128)S(1)} %copy-done.10, ...), custom_call_target="tpu_custom_call" | custom-call | tf_op jit(solution)/shard_map/pallas_call | solution.py:43
  22.7 0.7 copy-done.14
  23.4 22.6 %collective-permute-done.11.refs_4_ = bf16[1024,128]{1,0:T(8,128)(2,1)S(1)} collective-permute-done((bf16[1024,128]{1,0:T(8,128)(2,1)S(1)}, bf16[1024,128]{1,0:T(8,128)(2,1)S(1)}, u32[]{:S(2)}, u32[]{:S(2)}) %collective-permute-start.11) | collective-permute-done | bytes 262176 | tf_op jit(solution)/shard_map/ppermute | solution.py:327
  46.4 2.5 %collective-permute-start.9 = (bf16[1024,128]{1,0:T(8,128)(2,1)S(1)}, bf16[1024,128]{1,0:T(8,128)(2,1)S(1)}, u32[]{:S(2)}, u32[]{:S(2)}) collective-permute-start(bf16[1024,128]{1,0:T(8,128)(2,1)S(1)} %get-tuple-element.66), channel_id=1, source_target_pairs={{0,6},{1,7},{2,4},{3,5},{4,2},{5,3},{6,0},{7,1},{8,14},{9,15},{10,... | collective-permute-start | bytes 786440 | tf_op jit(solution)/shard_map/ppermute | solution.py:327
  48.9 1.3 %collective-permute-start.7 = (bf16[1024,128]{1,0:T(8,128)(2,1)S(1)}, bf16[1024,128]{1,0:T(8,128)(2,1)S(1)}, u32[]{:S(2)}, u32[]{:S(2)}) collective-permute-start(bf16[1024,128]{1,0:T(8,128)(2,1)S(1)} %get-tuple-element.60), channel_id=1, source_target_pairs={{0,2},{1,3},{2,0},{3,1},{4,6},{5,7},{6,4},{7,5},{8,10},{9,11},{10,... | collective-permute-start | bytes 786440 | tf_op jit(solution)/shard_map/ppermute | solution.py:327
  50.2 6.1 %collective-permute-done.3.refs_5_ = bf16[1024,128]{1,0:T(8,128)(2,1)S(1)} collective-permute-done((bf16[1024,128]{1,0:T(8,128)(2,1)S(1)}, bf16[1024,128]{1,0:T(8,128)(2,1)S(1)}, u32[]{:S(2)}, u32[]{:S(2)}) %collective-permute-start.3) | collective-permute-done | bytes 262176 | tf_op jit(solution)/shard_map/ppermute | solution.py:327
  56.4 2.1 %collective-permute-start.1 = (bf16[1024,128]{1,0:T(8,128)(2,1)S(1)}, bf16[1024,128]{1,0:T(8,128)(2,1)S(1)}, u32[]{:S(2)}, u32[]{:S(2)}) collective-permute-start(bf16[1024,128]{1,0:T(8,128)(2,1)S(1)} %get-tuple-element.47), channel_id=1, source_target_pairs={{0,3},{1,2},{2,1},{3,0},{4,7},{5,6},{6,5},{7,4},{8,11},{9,10},{10,... | collective-permute-start | bytes 786440 | tf_op jit(solution)/shard_map/ppermute | solution.py:327
  58.5 11.0 %collective-permute-done.12.refs_2_ = bf16[1024,128]{1,0:T(8,128)(2,1)S(1)} collective-permute-done((bf16[1024,128]{1,0:T(8,128)(2,1)S(1)}, bf16[1024,128]{1,0:T(8,128)(2,1)S(1)}, u32[]{:S(2)}, u32[]{:S(2)}) %collective-permute-start.12) | collective-permute-done | bytes 262176 | tf_op jit(solution)/shard_map/ppermute | solution.py:327
  69.6 2.3 %collective-permute-start.10 = (bf16[1024,128]{1,0:T(8,128)(2,1)}, bf16[1024,128]{1,0:T(8,128)(2,1)S(1)}, u32[]{:S(2)}, u32[]{:S(2)}) collective-permute-start(bf16[1024,128]{1,0:T(8,128)(2,1)} %get-tuple-element.67), channel_id=1, source_target_pairs={{0,12},{1,13},{2,14},{3,15},{4,8},{5,9},{6,10},{7,11},{8,4},{9,5},... | collective-permute-start | bytes 786440 | tf_op jit(solution)/shard_map/ppermute | solution.py:327
  72.1 12.8 %collective-permute-done.4.refs_3_ = bf16[1024,128]{1,0:T(8,128)(2,1)S(1)} collective-permute-done((bf16[1024,128]{1,0:T(8,128)(2,1)S(1)}, bf16[1024,128]{1,0:T(8,128)(2,1)S(1)}, u32[]{:S(2)}, u32[]{:S(2)}) %collective-permute-start.4) | collective-permute-done | bytes 262176 | tf_op jit(solution)/shard_map/ppermute | solution.py:327
  84.9 2.0 %collective-permute-start.5 = (bf16[1024,128]{1,0:T(8,128)(2,1)}, bf16[1024,128]{1,0:T(8,128)(2,1)S(1)}, u32[]{:S(2)}, u32[]{:S(2)}) collective-permute-start(bf16[1024,128]{1,0:T(8,128)(2,1)} %get-tuple-element.53), channel_id=1, source_target_pairs={{0,15},{1,14},{2,13},{3,12},{4,11},{5,10},{6,9},{7,8},{8,7},{9,6},... | collective-permute-start | bytes 786440 | tf_op jit(solution)/shard_map/ppermute | solution.py:327
  86.9 3.5 %collective-permute-start.2 = (bf16[1024,128]{1,0:T(8,128)(2,1)S(1)}, bf16[1024,128]{1,0:T(8,128)(2,1)S(1)}, u32[]{:S(2)}, u32[]{:S(2)}) collective-permute-start(bf16[1024,128]{1,0:T(8,128)(2,1)S(1)} %get-tuple-element.48), channel_id=1, source_target_pairs={{0,14},{1,15},{2,12},{3,13},{4,10},{5,11},{6,8},{7,9},{8,6},{9,7},... | collective-permute-start | bytes 786440 | tf_op jit(solution)/shard_map/ppermute | solution.py:327
  90.4 1.7 %shard_map.67 = (bf16[128,768]{1,0:T(8,128)(2,1)S(1)}, bf16[768,128]{1,0:T(8,128)(2,1)S(1)}, bf16[8,96,128]{2,1,0:T(8,128)(2,1)S(1)}) custom-call(s32[16]{0:T(128)S(1)} %copy-done.12, f32[48]{0:T(128)S(1)} %copy-done.13, bf16[16,144,128]{2,1,0:T(8,128)(2,1)S(1)} %all-to-all-done.matrix_ref), custom_call_target="tpu_custom_call" | custom-call | tf_op jit(solution)/shard_map/pallas_call | solution.py:146
  92.1 0.7 copy-done.2
  92.8 0.7 copy-done.4
  93.4 0.7 copy-done.6
  94.1 12.3 %shard_map.68.refs_7_ = bf16[128,128,128]{2,1,0:T(8,128)(2,1)} custom-call(bf16[1024,128]{1,0:T(8,128)(2,1)} %copy-done.14, bf16[1024,128]{1,0:T(8,128)(2,1)} %copy-done.17, bf16[1024,128]{1,0:T(8,128)(2,1)} %copy-done.16, bf16[1024,128]{1,0:T(8,128)(2,1)} %copy-done.19, bf16[1024,128]{1,0:T(8,128)(2,1)} %copy-done.15, bf16[1024,128]{1,0:T(8,128)(2,1)} %copy-done.18, ...), custom_call_target="tpu_custom_call" | custom-call | flops 3623878656 | bytes 25165824 | tf_op jit(solution)/shard_map/pallas_call | solution.py:286
  106.5 2.2 %copy-done.1 = bf16[128,128,128]{2,1,0:T(8,128)(2,1)S(1)} copy-done((bf16[128,128,128]{2,1,0:T(8,128)(2,1)S(1)}, bf16[128,128,128]{2,1,0:T(8,128)(2,1)}, u32[]{:S(2)}) %copy-start.1) | copy-done | bytes 4194328
  108.7 6.1 %shard_map.69.refs_7_ = bf16[128,128,128]{2,1,0:T(8,128)(2,1)S(1)} custom-call(bf16[1024,128]{1,0:T(8,128)(2,1)S(1)} %collective-permute-done.9.refs_0_, bf16[1024,128]{1,0:T(8,128)(2,1)S(1)} %collective-permute-done.14.refs_1_, bf16[1024,128]{1,0:T(8,128)(2,1)S(1)} %collective-permute-done.12.refs_2_, bf16[1024,128]{1,0:T(8,128)(2,1)S(1)} %collective-permute-done.4.refs_3_, ...), custom_call_target="tpu_custom_call" | custom-call | flops 2415919104 | bytes 25165824 | tf_op jit(solution)/shard_map/pallas_call | solution.py:286
  114.8 6.2 %shard_map.70.refs_5_ = bf16[128,128,128]{2,1,0:T(8,128)(2,1)S(1)} custom-call(bf16[1024,128]{1,0:T(8,128)(2,1)S(1)} %collective-permute-done.7.refs_0_, bf16[1024,128]{1,0:T(8,128)(2,1)S(1)} %collective-permute-done.1.refs_1_, bf16[1024,128]{1,0:T(8,128)(2,1)S(1)} %collective-permute-done.10.refs_2_, bf16[1024,128]{1,0:T(8,128)(2,1)S(1)} %collective-permute-done.13.refs_3_, ...), custom_call_target="tpu_custom_call" | custom-call | flops 2415919104 | bytes 25165824 | tf_op jit(solution)/shard_map/pallas_call | solution.py:286
  121.0 6.5 %shard_map.71 = bf16[128,128,128]{2,1,0:T(8,128)(2,1)} custom-call(bf16[1024,128]{1,0:T(8,128)(2,1)S(1)} %collective-permute-done.2.refs_0_, bf16[1024,128]{1,0:T(8,128)(2,1)S(1)} %collective-permute-done.5.refs_1_, bf16[128,768]{1,0:T(8,128)(2,1)S(1)} %copy-done.3, bf16[768,128]{1,0:T(8,128)(2,1)S(1)} %copy-done.5, bf16[8,96,128]{2,1,0:T(8,128)(2,1)S(1)} %copy-done.7, ...), custom_call_target="tpu_custom_call" | custom-call | flops 1207959552 | bytes 25165824 | tf_op jit(solution)/shard_map/pallas_call | solution.py:286
  (48 shorter events, 0.9 us)
Async XLA Ops:
  0.0 0.9 copy-start.8
  0.9 0.7 copy-start.9
  4.5 85.9 %all-to-all-start = ((bf16[16,144,128]{2,1,0:T(8,128)(2,1)}), bf16[16,144,128]{2,1,0:T(8,128)(2,1)S(1)}, u32[]{:S(2)}, u32[]{:S(2)}) async-start(bf16[16,144,128]{2,1,0:T(8,128)(2,1)} %shard_map.66), calls=%async_computation | async-start | bytes 1179648 | tf_op jit(solution)/shard_map/all_to_all | solution.py:332
  11.9 2.2 %copy-start = (bf16[16,1024,128]{2,1,0:T(8,128)(2,1)S(1)}, bf16[16,1024,128]{2,1,0:T(8,128)(2,1)}, u32[]{:S(2)}) copy-start(bf16[16,1024,128]{2,1,0:T(8,128)(2,1)} %source_ref.3) | copy-start | bytes 12582916
  14.7 75.7 %copy-start.12 = (s32[16]{0:T(128)S(1)}, s32[16]{0:T(128)}, u32[]{:S(2)}) copy-start(s32[16]{0:T(128)} %counts_ref.3) | copy-start | bytes 196
  14.7 75.7 %copy-start.13 = (f32[48]{0:T(128)S(1)}, f32[48]{0:T(128)}, u32[]{:S(2)}) copy-start(f32[48]{0:T(128)} %weights_ref.1) | copy-start | bytes 580
  15.6 30.4 %collective-permute-start.11 = (bf16[1024,128]{1,0:T(8,128)(2,1)S(1)}, bf16[1024,128]{1,0:T(8,128)(2,1)S(1)}, u32[]{:S(2)}, u32[]{:S(2)}) collective-permute-start(bf16[1024,128]{1,0:T(8,128)(2,1)S(1)} %get-tuple-element.70), channel_id=1, source_target_pairs={{0,8},{1,9},{2,10},{3,11},{4,12},{5,13},{6,14},{7,15},{8,0},{9,1},... | collective-permute-start | bytes 786440 | tf_op jit(solution)/shard_map/ppermute | solution.py:327
  18.5 27.9 %collective-permute-start.8 = (bf16[1024,128]{1,0:T(8,128)(2,1)S(1)}, bf16[1024,128]{1,0:T(8,128)(2,1)S(1)}, u32[]{:S(2)}, u32[]{:S(2)}) collective-permute-start(bf16[1024,128]{1,0:T(8,128)(2,1)S(1)} %get-tuple-element.65), channel_id=1, source_target_pairs={{0,4},{1,5},{2,6},{3,7},{4,0},{5,1},{6,2},{7,3},{8,12},{9,13},{10,... | collective-permute-start | bytes 786440 | tf_op jit(solution)/shard_map/ppermute | solution.py:327
  19.9 29.0 %collective-permute-start.6 = (bf16[1024,128]{1,0:T(8,128)(2,1)S(1)}, bf16[1024,128]{1,0:T(8,128)(2,1)S(1)}, u32[]{:S(2)}, u32[]{:S(2)}) collective-permute-start(bf16[1024,128]{1,0:T(8,128)(2,1)S(1)} %get-tuple-element.59), channel_id=1, source_target_pairs={{0,1},{1,0},{2,3},{3,2},{4,5},{5,4},{6,7},{7,6},{8,9},{9,8},{10,11... | collective-permute-start | bytes 786440 | tf_op jit(solution)/shard_map/ppermute | solution.py:327
  19.9 36.4 %collective-permute-start.3 = (bf16[1024,128]{1,0:T(8,128)(2,1)S(1)}, bf16[1024,128]{1,0:T(8,128)(2,1)S(1)}, u32[]{:S(2)}, u32[]{:S(2)}) collective-permute-start(bf16[1024,128]{1,0:T(8,128)(2,1)S(1)} %get-tuple-element.51), channel_id=1, source_target_pairs={{0,9},{1,8},{2,11},{3,10},{4,13},{5,12},{6,15},{7,14},{8,1},{9,0},... | collective-permute-start | bytes 786440 | tf_op jit(solution)/shard_map/ppermute | solution.py:327
  20.6 35.7 %collective-permute-start = (bf16[1024,128]{1,0:T(8,128)(2,1)S(1)}, bf16[1024,128]{1,0:T(8,128)(2,1)S(1)}, u32[]{:S(2)}, u32[]{:S(2)}) collective-permute-start(bf16[1024,128]{1,0:T(8,128)(2,1)S(1)} %get-tuple-element.46), channel_id=1, source_target_pairs={{0,5},{1,4},{2,7},{3,6},{4,1},{5,0},{6,3},{7,2},{8,13},{9,12},{10,... | collective-permute-start | bytes 786440 | tf_op jit(solution)/shard_map/ppermute | solution.py:327
  22.7 0.7 copy-start.14
  45.9 10.4 %copy-start.15 = (bf16[1024,128]{1,0:T(8,128)(2,1)}, bf16[1024,128]{1,0:T(8,128)(2,1)S(1)}, u32[]{:S(2)}) copy-start(bf16[1024,128]{1,0:T(8,128)(2,1)S(1)} %collective-permute-done.11.refs_4_) | copy-start | bytes 786436
  45.9 23.5 %collective-permute-start.12 = (bf16[1024,128]{1,0:T(8,128)(2,1)S(1)}, bf16[1024,128]{1,0:T(8,128)(2,1)S(1)}, u32[]{:S(2)}, u32[]{:S(2)}) collective-permute-start(bf16[1024,128]{1,0:T(8,128)(2,1)S(1)} %get-tuple-element.71), channel_id=1, source_target_pairs={{0,10},{1,11},{2,8},{3,9},{4,14},{5,15},{6,12},{7,13},{8,2},{9,3},... | collective-permute-start | bytes 786440 | tf_op jit(solution)/shard_map/ppermute | solution.py:327
  46.4 23.0 %copy-start.16 = (bf16[1024,128]{1,0:T(8,128)(2,1)}, bf16[1024,128]{1,0:T(8,128)(2,1)S(1)}, u32[]{:S(2)}) copy-start(bf16[1024,128]{1,0:T(8,128)(2,1)S(1)} %collective-permute-done.8.refs_2_) | copy-start | bytes 786436
  46.4 23.2 %collective-permute-start.9 = (bf16[1024,128]{1,0:T(8,128)(2,1)S(1)}, bf16[1024,128]{1,0:T(8,128)(2,1)S(1)}, u32[]{:S(2)}, u32[]{:S(2)}) collective-permute-start(bf16[1024,128]{1,0:T(8,128)(2,1)S(1)} %get-tuple-element.66), channel_id=1, source_target_pairs={{0,6},{1,7},{2,4},{3,5},{4,2},{5,3},{6,0},{7,1},{8,14},{9,15},{10,... | collective-permute-start | bytes 786440 | tf_op jit(solution)/shard_map/ppermute | solution.py:327
  48.9 20.7 %copy-start.17 = (bf16[1024,128]{1,0:T(8,128)(2,1)}, bf16[1024,128]{1,0:T(8,128)(2,1)S(1)}, u32[]{:S(2)}) copy-start(bf16[1024,128]{1,0:T(8,128)(2,1)S(1)} %collective-permute-done.6.refs_1_) | copy-start | bytes 786436
  48.9 23.0 %collective-permute-start.7 = (bf16[1024,128]{1,0:T(8,128)(2,1)S(1)}, bf16[1024,128]{1,0:T(8,128)(2,1)S(1)}, u32[]{:S(2)}, u32[]{:S(2)}) collective-permute-start(bf16[1024,128]{1,0:T(8,128)(2,1)S(1)} %get-tuple-element.60), channel_id=1, source_target_pairs={{0,2},{1,3},{2,0},{3,1},{4,6},{5,7},{6,4},{7,5},{8,10},{9,11},{10,... | collective-permute-start | bytes 786440 | tf_op jit(solution)/shard_map/ppermute | solution.py:327
  56.3 28.5 %copy-start.18 = (bf16[1024,128]{1,0:T(8,128)(2,1)}, bf16[1024,128]{1,0:T(8,128)(2,1)S(1)}, u32[]{:S(2)}) copy-start(bf16[1024,128]{1,0:T(8,128)(2,1)S(1)} %collective-permute-done.3.refs_5_) | copy-start | bytes 786436
  56.3 28.5 %collective-permute-start.4 = (bf16[1024,128]{1,0:T(8,128)(2,1)S(1)}, bf16[1024,128]{1,0:T(8,128)(2,1)S(1)}, u32[]{:S(2)}, u32[]{:S(2)}) collective-permute-start(bf16[1024,128]{1,0:T(8,128)(2,1)S(1)} %get-tuple-element.52), channel_id=1, source_target_pairs={{0,11},{1,10},{2,9},{3,8},{4,15},{5,14},{6,13},{7,12},{8,3},{9,2},... | collective-permute-start | bytes 786440 | tf_op jit(solution)/shard_map/ppermute | solution.py:327
  56.4 30.6 %copy-start.19 = (bf16[1024,128]{1,0:T(8,128)(2,1)}, bf16[1024,128]{1,0:T(8,128)(2,1)S(1)}, u32[]{:S(2)}) copy-start(bf16[1024,128]{1,0:T(8,128)(2,1)S(1)} %collective-permute-done.refs_3_) | copy-start | bytes 786436
  56.4 30.5 %collective-permute-start.1 = (bf16[1024,128]{1,0:T(8,128)(2,1)S(1)}, bf16[1024,128]{1,0:T(8,128)(2,1)S(1)}, u32[]{:S(2)}, u32[]{:S(2)}) collective-permute-start(bf16[1024,128]{1,0:T(8,128)(2,1)S(1)} %get-tuple-element.47), channel_id=1, source_target_pairs={{0,3},{1,2},{2,1},{3,0},{4,7},{5,6},{6,5},{7,4},{8,11},{9,10},{10,... | collective-permute-start | bytes 786440 | tf_op jit(solution)/shard_map/ppermute | solution.py:327
  69.4 45.4 %collective-permute-start.13 = (bf16[1024,128]{1,0:T(8,128)(2,1)}, bf16[1024,128]{1,0:T(8,128)(2,1)S(1)}, u32[]{:S(2)}, u32[]{:S(2)}) collective-permute-start(bf16[1024,128]{1,0:T(8,128)(2,1)} %get-tuple-element.72), channel_id=1, source_target_pairs={{0,13},{1,12},{2,15},{3,14},{4,9},{5,8},{6,11},{7,10},{8,5},{9,4},... | collective-permute-start | bytes 786440 | tf_op jit(solution)/shard_map/ppermute | solution.py:327
  69.6 45.2 %collective-permute-start.10 = (bf16[1024,128]{1,0:T(8,128)(2,1)}, bf16[1024,128]{1,0:T(8,128)(2,1)S(1)}, u32[]{:S(2)}, u32[]{:S(2)}) collective-permute-start(bf16[1024,128]{1,0:T(8,128)(2,1)} %get-tuple-element.67), channel_id=1, source_target_pairs={{0,12},{1,13},{2,14},{3,15},{4,8},{5,9},{6,10},{7,11},{8,4},{9,5},... | collective-permute-start | bytes 786440 | tf_op jit(solution)/shard_map/ppermute | solution.py:327
  71.9 34.5 %collective-permute-start.14 = (bf16[1024,128]{1,0:T(8,128)(2,1)}, bf16[1024,128]{1,0:T(8,128)(2,1)S(1)}, u32[]{:S(2)}, u32[]{:S(2)}) collective-permute-start(bf16[1024,128]{1,0:T(8,128)(2,1)} %get-tuple-element.74), channel_id=1, source_target_pairs={{0,7},{1,6},{2,5},{3,4},{4,3},{5,2},{6,1},{7,0},{8,15},{9,14},{10,... | collective-permute-start | bytes 786440 | tf_op jit(solution)/shard_map/ppermute | solution.py:327
  84.9 36.1 %collective-permute-start.5 = (bf16[1024,128]{1,0:T(8,128)(2,1)}, bf16[1024,128]{1,0:T(8,128)(2,1)S(1)}, u32[]{:S(2)}, u32[]{:S(2)}) collective-permute-start(bf16[1024,128]{1,0:T(8,128)(2,1)} %get-tuple-element.53), channel_id=1, source_target_pairs={{0,15},{1,14},{2,13},{3,12},{4,11},{5,10},{6,9},{7,8},{8,7},{9,6},... | collective-permute-start | bytes 786440 | tf_op jit(solution)/shard_map/ppermute | solution.py:327
  86.9 34.1 %collective-permute-start.2 = (bf16[1024,128]{1,0:T(8,128)(2,1)S(1)}, bf16[1024,128]{1,0:T(8,128)(2,1)S(1)}, u32[]{:S(2)}, u32[]{:S(2)}) collective-permute-start(bf16[1024,128]{1,0:T(8,128)(2,1)S(1)} %get-tuple-element.48), channel_id=1, source_target_pairs={{0,14},{1,15},{2,12},{3,13},{4,10},{5,11},{6,8},{7,9},{8,6},{9,7},... | collective-permute-start | bytes 786440 | tf_op jit(solution)/shard_map/ppermute | solution.py:327
  93.4 0.7 copy-start.6
  94.1 12.3 %copy-start.3 = (bf16[128,768]{1,0:T(8,128)(2,1)S(1)}, bf16[128,768]{1,0:T(8,128)(2,1)}, u32[]{:S(2)}) copy-start(bf16[128,768]{1,0:T(8,128)(2,1)} %copy-done.2) | copy-start | bytes 589828
  94.1 12.3 %copy-start.5 = (bf16[768,128]{1,0:T(8,128)(2,1)S(1)}, bf16[768,128]{1,0:T(8,128)(2,1)}, u32[]{:S(2)}) copy-start(bf16[768,128]{1,0:T(8,128)(2,1)} %copy-done.4) | copy-start | bytes 589828
  94.1 12.3 %copy-start.7 = (bf16[8,96,128]{2,1,0:T(8,128)(2,1)S(1)}, bf16[8,96,128]{2,1,0:T(8,128)(2,1)}, u32[]{:S(2)}) copy-start(bf16[8,96,128]{2,1,0:T(8,128)(2,1)} %copy-done.6) | copy-start | bytes 589828
  106.5 2.2 %copy-start.1 = (bf16[128,128,128]{2,1,0:T(8,128)(2,1)S(1)}, bf16[128,128,128]{2,1,0:T(8,128)(2,1)}, u32[]{:S(2)}) copy-start(bf16[128,128,128]{2,1,0:T(8,128)(2,1)} %shard_map.68.refs_7_) | copy-start | bytes 12582916
  (4 other events, 2.6 us)

commit v2 on v1

--- a/solution.py
+++ b/solution.py
@@ -17,7 +17,6 @@
 FAR_TURNS = (2, 4)
 SMALL_VMEM = 16 * 1024 * 1024
 ROOM = 13 * 1024 * 1024
-FIRST_VMEM = 60 * 1024 * 1024
 
 
 def pieces_kernel(shifts, ids_ref, source_ref, *refs):
@@ -291,7 +290,7 @@
         out_shape=out_shape,
         scratch_shapes=scratch,
         compiler_params=pltpu.CompilerParams(
-            dimension_semantics=("arbitrary",), vmem_limit_bytes=FIRST_VMEM if first else ROOM + 4 * extent * extent * (depth + 8)
+            dimension_semantics=("arbitrary",), vmem_limit_bytes=ROOM + 4 * extent * extent * (depth + 8)
         ),
         cost_estimate=pl.CostEstimate(
             flops=6 * MOST * rows * extent * extent,
@@ -331,13 +330,16 @@
     matrices = choose_matrices(perambs, peramb_ids, sink_counts, workers, extent)
     matrices = lax.all_to_all(matrices, "work", split_axis=0, concat_axis=0, tiled=True)
     leg3, leg2, leg1 = make_legs(matrices, sink_counts, weights, workers)
-    for place in range(IN_FLIGHT, len(order)):
+    for place in range(IN_FLIGHT, len(order) - 1):
         send(place)
 
     acc = None
     for group, units in enumerate(GROUPS):
         members = [arrived[u * per_unit + lane] for u in units for lane in range(per_unit)]
         acc = add_group(units, members, leg3, leg2, leg1, acc, group == len(GROUPS) - 1)
+        if group == 0:
+            pieces[order[-1]], acc = lax.optimization_barrier((pieces[order[-1]], acc))
+            send(len(order) - 1)
     return acc.reshape(1, extent * extent, extent)
 
 

time: 128 us -> 128 us (level)
  the two profiles are of different devices: /device:TPU:0 before, /device:TPU:11 now
where the time goes in v2:
time: 128 us
  waiting for transfers between devices  46.1 us (36%)
  Pallas kernels  34.7 us (27%)
  starting transfers between devices  31.5 us (25%)
  local copies, waits for them, and re-layouts  15 us (12%)
    ppermute x15, waiting for transfers between devices, send(): lax.ppermute(piece, 'work', [(i, i ^ shift) for i in range(workers)])  46.1 us
    pallas_call x4, Pallas kernels, add_group(): pl.pallas_call(functools.partial(group_kernel, first, last, units, per_un...  27.9 us
    ppermute x15, starting transfers between devices, send(): lax.ppermute(piece, 'work', [(i, i ^ shift) for i in range(workers)])  24.9 us
    unnamed x38, local copies, waits for them, and re-layouts  15 us
    all_to_all x1, starting transfers between devices, per_device(): lax.all_to_all(matrices, 'work', split_axis=0, concat_axis=0, tiled=True)  6.61 us
    pallas_call x2, Pallas kernels, choose_pieces(): pl.pallas_call(functools.partial(pieces_kernel, shifts), in_specs=[pl.Blo...  2.92 us
  transfers between devices with their start and end apart: 16, of which 7 were waited for; matrix products, arithmetic and copies ran while one was open for 0% of the time, Pallas kernels for 20%

profile of v2, /device:TPU:11, one launch (start us, length us, event | category | flops | bytes accessed | tf_op | source)
XLA Modules:
  0.0 127.6 jit_solution(17582719878501448359)
XLA Ops:
  2.3 2.2 %shard_map.66 = bf16[16,144,128]{2,1,0:T(8,128)(2,1)} custom-call(s32[16]{0:T(128)S(1)} %copy-done.4, s32[3,48]{1,0:T(4,128)S(1)} %bitcast.2, bf16[96,1024]{1,0:T(8,128)(2,1)S(1)} %copy-done.1), custom_call_target="tpu_custom_call" | custom-call | tf_op jit(solution)/shard_map/pallas_call | solution.py:89
  4.5 6.6 %all-to-all-start = ((bf16[16,144,128]{2,1,0:T(8,128)(2,1)}), bf16[16,144,128]{2,1,0:T(8,128)(2,1)S(1)}, u32[]{:S(2)}, u32[]{:S(2)}) async-start(bf16[16,144,128]{2,1,0:T(8,128)(2,1)} %shard_map.66), calls=%async_computation | async-start | bytes 1179648 | tf_op jit(solution)/shard_map/all_to_all | solution.py:331
  11.1 2.2 %copy-done = bf16[16,1024,128]{2,1,0:T(8,128)(2,1)S(1)} copy-done((bf16[16,1024,128]{2,1,0:T(8,128)(2,1)S(1)}, bf16[16,1024,128]{2,1,0:T(8,128)(2,1)}, u32[]{:S(2)}) %copy-start) | copy-done | bytes 4194328
  15.4 1.4 %collective-permute-start.4 = (bf16[1024,128]{1,0:T(8,128)(2,1)S(1)}, bf16[1024,128]{1,0:T(8,128)(2,1)S(1)}, u32[]{:S(2)}, u32[]{:S(2)}) collective-permute-start(bf16[1024,128]{1,0:T(8,128)(2,1)S(1)} %get-tuple-element.57), channel_id=1, source_target_pairs={{0,4},{1,5},{2,6},{3,7},{4,0},{5,1},{6,2},{7,3},{8,12},{9,13},{10,... | collective-permute-start | bytes 786440 | tf_op jit(solution)/shard_map/ppermute | solution.py:326
  16.7 2.1 %collective-permute-start.5 = (bf16[1024,128]{1,0:T(8,128)(2,1)S(1)}, bf16[1024,128]{1,0:T(8,128)(2,1)S(1)}, u32[]{:S(2)}, u32[]{:S(2)}) collective-permute-start(bf16[1024,128]{1,0:T(8,128)(2,1)S(1)} %get-tuple-element.61), channel_id=1, source_target_pairs={{0,8},{1,9},{2,10},{3,11},{4,12},{5,13},{6,14},{7,15},{8,0},{9,1},... | collective-permute-start | bytes 786440 | tf_op jit(solution)/shard_map/ppermute | solution.py:326
  18.8 1.1 collective-permute-start.6
  19.9 2.1 %shard_map.64 = (bf16[1024,128]{1,0:T(8,128)(2,1)S(1)}, bf16[1024,128]{1,0:T(8,128)(2,1)S(1)}, bf16[1024,128]{1,0:T(8,128)(2,1)S(1)}, bf16[1024,128]{1,0:T(8,128...) custom-call(s32[16]{0:T(128)S(1)} %copy-done.3, ...), custom_call_target="tpu_custom_call" | custom-call | tf_op jit(solution)/shard_map/pallas_call | solution.py:42
  22.7 12.7 %collective-permute-done.refs_3_ = bf16[1024,128]{1,0:T(8,128)(2,1)S(1)} collective-permute-done((bf16[1024,128]{1,0:T(8,128)(2,1)S(1)}, bf16[1024,128]{1,0:T(8,128)(2,1)S(1)}, u32[]{:S(2)}, u32[]{:S(2)}) %collective-permute-start) | collective-permute-done | bytes 262176 | tf_op jit(solution)/shard_map/ppermute | solution.py:326
  36.1 2.5 %collective-permute-start.1 = (bf16[1024,128]{1,0:T(8,128)(2,1)S(1)}, bf16[1024,128]{1,0:T(8,128)(2,1)S(1)}, u32[]{:S(2)}, u32[]{:S(2)}) collective-permute-start(bf16[1024,128]{1,0:T(8,128)(2,1)S(1)} %get-tuple-element.49), channel_id=1, source_target_pairs={{0,3},{1,2},{2,1},{3,0},{4,7},{5,6},{6,5},{7,4},{8,11},{9,10},{10,... | collective-permute-start | bytes 786440 | tf_op jit(solution)/shard_map/ppermute | solution.py:326
  39.7 1.5 %collective-permute-done.4.refs_2_ = bf16[1024,128]{1,0:T(8,128)(2,1)S(1)} collective-permute-done((bf16[1024,128]{1,0:T(8,128)(2,1)S(1)}, bf16[1024,128]{1,0:T(8,128)(2,1)S(1)}, u32[]{:S(2)}, u32[]{:S(2)}) %collective-permute-start.4) | collective-permute-done | bytes 262176 | tf_op jit(solution)/shard_map/ppermute | solution.py:326
  41.9 3.1 %collective-permute-start.10 = (bf16[1024,128]{1,0:T(8,128)(2,1)S(1)}, bf16[1024,128]{1,0:T(8,128)(2,1)S(1)}, u32[]{:S(2)}, u32[]{:S(2)}) collective-permute-start(bf16[1024,128]{1,0:T(8,128)(2,1)S(1)} %get-tuple-element.77), channel_id=1, source_target_pairs={{0,6},{1,7},{2,4},{3,5},{4,2},{5,3},{6,0},{7,1},{8,14},{9,15},{10,... | collective-permute-start | bytes 786440 | tf_op jit(solution)/shard_map/ppermute | solution.py:326
  45.7 1.5 %collective-permute-done.6.refs_5_ = bf16[1024,128]{1,0:T(8,128)(2,1)S(1)} collective-permute-done((bf16[1024,128]{1,0:T(8,128)(2,1)S(1)}, bf16[1024,128]{1,0:T(8,128)(2,1)S(1)}, u32[]{:S(2)}, u32[]{:S(2)}) %collective-permute-start.6) | collective-permute-done | bytes 262176 | tf_op jit(solution)/shard_map/ppermute | solution.py:326
  47.9 3.6 %collective-permute-start.7 = (bf16[1024,128]{1,0:T(8,128)(2,1)}, bf16[1024,128]{1,0:T(8,128)(2,1)S(1)}, u32[]{:S(2)}, u32[]{:S(2)}) collective-permute-start(bf16[1024,128]{1,0:T(8,128)(2,1)} %get-tuple-element.70), channel_id=1, source_target_pairs={{0,11},{1,10},{2,9},{3,8},{4,15},{5,14},{6,13},{7,12},{8,3},{9,2},... | collective-permute-start | bytes 786440 | tf_op jit(solution)/shard_map/ppermute | solution.py:326
  51.6 1.2 collective-permute-start.2
  52.8 15.4 %collective-permute-done.9.refs_0_ = bf16[1024,128]{1,0:T(8,128)(2,1)S(1)} collective-permute-done((bf16[1024,128]{1,0:T(8,128)(2,1)S(1)}, bf16[1024,128]{1,0:T(8,128)(2,1)S(1)}, u32[]{:S(2)}, u32[]{:S(2)}) %collective-permute-start.9) | collective-permute-done | bytes 262176 | tf_op jit(solution)/shard_map/ppermute | solution.py:326
  68.2 6.5 %collective-permute-done.12.refs_2_ = bf16[1024,128]{1,0:T(8,128)(2,1)S(1)} collective-permute-done((bf16[1024,128]{1,0:T(8,128)(2,1)S(1)}, bf16[1024,128]{1,0:T(8,128)(2,1)S(1)}, u32[]{:S(2)}, u32[]{:S(2)}) %collective-permute-start.12) | collective-permute-done | bytes 262176 | tf_op jit(solution)/shard_map/ppermute | solution.py:326
  74.7 2.4 %collective-permute-start.13 = (bf16[1024,128]{1,0:T(8,128)(2,1)}, bf16[1024,128]{1,0:T(8,128)(2,1)S(1)}, u32[]{:S(2)}, u32[]{:S(2)}) collective-permute-start(bf16[1024,128]{1,0:T(8,128)(2,1)} %get-tuple-element.81), channel_id=1, source_target_pairs={{0,13},{1,12},{2,15},{3,14},{4,9},{5,8},{6,11},{7,10},{8,5},{9,4},... | collective-permute-start | bytes 786440 | tf_op jit(solution)/shard_map/ppermute | solution.py:326
  77.1 3.0 %collective-permute-start.14 = (bf16[1024,128]{1,0:T(8,128)(2,1)}, bf16[1024,128]{1,0:T(8,128)(2,1)S(1)}, u32[]{:S(2)}, u32[]{:S(2)}) collective-permute-start(bf16[1024,128]{1,0:T(8,128)(2,1)} %get-tuple-element.83), channel_id=1, source_target_pairs={{0,7},{1,6},{2,5},{3,4},{4,3},{5,2},{6,1},{7,0},{8,15},{9,14},{10,... | collective-permute-start | bytes 786440 | tf_op jit(solution)/shard_map/ppermute | solution.py:326
  80.2 1.7 %shard_map.67 = (bf16[128,768]{1,0:T(8,128)(2,1)S(1)}, bf16[768,128]{1,0:T(8,128)(2,1)S(1)}, bf16[8,96,128]{2,1,0:T(8,128)(2,1)S(1)}) custom-call(s32[16]{0:T(128)S(1)} %copy-done.5, f32[48]{0:T(128)S(1)} %copy-done.6, bf16[16,144,128]{2,1,0:T(8,128)(2,1)S(1)} %all-to-all-done.matrix_ref), custom_call_target="tpu_custom_call" | custom-call | tf_op jit(solution)/shard_map/pallas_call | solution.py:145
  81.9 0.9 copy-done.8
  82.8 0.9 copy-done.10
  83.8 0.9 copy-done.12
  84.7 0.9 copy-done.14
  85.7 0.9 copy-done.16
  86.6 0.9 copy-done.18
  87.6 9.2 %shard_map.68.refs_7_ = bf16[128,128,128]{2,1,0:T(8,128)(2,1)S(1)} custom-call(bf16[1024,128]{1,0:T(8,128)(2,1)S(1)} %copy-done.18, bf16[1024,128]{1,0:T(8,128)(2,1)S(1)} %copy-done.10, bf16[1024,128]{1,0:T(8,128)(2,1)S(1)} %copy-done.12, bf16[1024,128]{1,0:T(8,128)(2,1)S(1)} %copy-done.8, bf16[1024,128]{1,0:T(8,128)(2,1)S(1)} %copy-done.14, ...), custom_call_target="tpu_custom_call" | custom-call | flops 3623878656 | bytes 25165824 | tf_op jit(solution)/shard_map/pallas_call | solution.py:285
  96.7 3.5 %collective-permute-start.8 = (bf16[1024,128]{1,0:T(8,128)(2,1)S(1)}, bf16[1024,128]{1,0:T(8,128)(2,1)S(1)}, u32[]{:S(2)}, u32[]{:S(2)}) collective-permute-start(bf16[1024,128]{1,0:T(8,128)(2,1)S(1)} %get-tuple-element.71), channel_id=1, source_target_pairs={{0,15},{1,14},{2,13},{3,12},{4,11},{5,10},{6,9},{7,8},{8,7},{9,6},... | collective-permute-start | bytes 786440 | tf_op jit(solution)/shard_map/ppermute | solution.py:326
  100.2 6.1 %shard_map.69.refs_7_ = bf16[128,128,128]{2,1,0:T(8,128)(2,1)S(1)} custom-call(bf16[1024,128]{1,0:T(8,128)(2,1)S(1)} %collective-permute-done.10.refs_0_, bf16[1024,128]{1,0:T(8,128)(2,1)S(1)} %collective-permute-done.14.refs_1_, bf16[1024,128]{1,0:T(8,128)(2,1)S(1)} %collective-permute-done.12.refs_2_, ...), custom_call_target="tpu_custom_call" | custom-call | flops 2415919104 | bytes 25165824 | tf_op jit(solution)/shard_map/pallas_call | solution.py:285
  106.4 2.1 %collective-permute-done.11.refs_2_ = bf16[1024,128]{1,0:T(8,128)(2,1)S(1)} collective-permute-done((bf16[1024,128]{1,0:T(8,128)(2,1)}, bf16[1024,128]{1,0:T(8,128)(2,1)S(1)}, u32[]{:S(2)}, u32[]{:S(2)}) %collective-permute-start.11) | collective-permute-done | bytes 262176 | tf_op jit(solution)/shard_map/ppermute | solution.py:326
  108.5 6.3 %collective-permute-done.13.refs_3_ = bf16[1024,128]{1,0:T(8,128)(2,1)S(1)} collective-permute-done((bf16[1024,128]{1,0:T(8,128)(2,1)}, bf16[1024,128]{1,0:T(8,128)(2,1)S(1)}, u32[]{:S(2)}, u32[]{:S(2)}) %collective-permute-start.13) | collective-permute-done | bytes 262176 | tf_op jit(solution)/shard_map/ppermute | solution.py:326
  114.8 6.1 %shard_map.70.refs_5_ = bf16[128,128,128]{2,1,0:T(8,128)(2,1)S(1)} custom-call(bf16[1024,128]{1,0:T(8,128)(2,1)S(1)} %collective-permute-done.9.refs_0_, bf16[1024,128]{1,0:T(8,128)(2,1)S(1)} %collective-permute-done.1.refs_1_, bf16[1024,128]{1,0:T(8,128)(2,1)S(1)} %collective-permute-done.11.refs_2_, bf16[1024,128]{1,0:T(8,128)(2,1)S(1)} %collective-permute-done.13.refs_3_, ...), custom_call_target="tpu_custom_call" | custom-call | flops 2415919104 | bytes 25165824 | tf_op jit(solution)/shard_map/pallas_call | solution.py:285
  121.0 6.5 %shard_map.71 = bf16[128,128,128]{2,1,0:T(8,128)(2,1)} custom-call(bf16[1024,128]{1,0:T(8,128)(2,1)S(1)} %collective-permute-done.2.refs_0_, bf16[1024,128]{1,0:T(8,128)(2,1)S(1)} %collective-permute-done.8.refs_1_, bf16[128,768]{1,0:T(8,128)(2,1)S(1)} %get-tuple-element.66.refs_6_.refs_4_.refs_2_, ...), custom_call_target="tpu_custom_call" | custom-call | flops 1207959552 | bytes 25165824 | tf_op jit(solution)/shard_map/pallas_call | solution.py:285
  (46 shorter events, 9.0 us)
Async XLA Ops:
  0.0 0.9 copy-start.1
  4.5 75.7 %all-to-all-start = ((bf16[16,144,128]{2,1,0:T(8,128)(2,1)}), bf16[16,144,128]{2,1,0:T(8,128)(2,1)S(1)}, u32[]{:S(2)}, u32[]{:S(2)}) async-start(bf16[16,144,128]{2,1,0:T(8,128)(2,1)} %shard_map.66), calls=%async_computation | async-start | bytes 1179648 | tf_op jit(solution)/shard_map/all_to_all | solution.py:331
  11.1 2.2 %copy-start = (bf16[16,1024,128]{2,1,0:T(8,128)(2,1)S(1)}, bf16[16,1024,128]{2,1,0:T(8,128)(2,1)}, u32[]{:S(2)}) copy-start(bf16[16,1024,128]{2,1,0:T(8,128)(2,1)} %source_ref.3) | copy-start | bytes 12582916
  13.9 66.2 %copy-start.5 = (s32[16]{0:T(128)S(1)}, s32[16]{0:T(128)}, u32[]{:S(2)}) copy-start(s32[16]{0:T(128)} %counts_ref.3) | copy-start | bytes 196
  13.9 66.2 %copy-start.6 = (f32[48]{0:T(128)S(1)}, f32[48]{0:T(128)}, u32[]{:S(2)}) copy-start(f32[48]{0:T(128)} %weights_ref.1) | copy-start | bytes 580
  14.8 20.6 %collective-permute-start = (bf16[1024,128]{1,0:T(8,128)(2,1)S(1)}, bf16[1024,128]{1,0:T(8,128)(2,1)S(1)}, u32[]{:S(2)}, u32[]{:S(2)}) collective-permute-start(bf16[1024,128]{1,0:T(8,128)(2,1)S(1)} %get-tuple-element.48), channel_id=1, source_target_pairs={{0,5},{1,4},{2,7},{3,6},{4,1},{5,0},{6,3},{7,2},{8,13},{9,12},{10,... | collective-permute-start | bytes 786440 | tf_op jit(solution)/shard_map/ppermute | solution.py:326
  14.9 23.7 %collective-permute-start.3 = (bf16[1024,128]{1,0:T(8,128)(2,1)S(1)}, bf16[1024,128]{1,0:T(8,128)(2,1)S(1)}, u32[]{:S(2)}, u32[]{:S(2)}) collective-permute-start(bf16[1024,128]{1,0:T(8,128)(2,1)S(1)} %get-tuple-element.54), channel_id=1, source_target_pairs={{0,1},{1,0},{2,3},{3,2},{4,5},{5,4},{6,7},{7,6},{8,9},{9,8},{10,11... | collective-permute-start | bytes 786440 | tf_op jit(solution)/shard_map/ppermute | solution.py:326
  15.4 25.8 %collective-permute-start.4 = (bf16[1024,128]{1,0:T(8,128)(2,1)S(1)}, bf16[1024,128]{1,0:T(8,128)(2,1)S(1)}, u32[]{:S(2)}, u32[]{:S(2)}) collective-permute-start(bf16[1024,128]{1,0:T(8,128)(2,1)S(1)} %get-tuple-element.57), channel_id=1, source_target_pairs={{0,4},{1,5},{2,6},{3,7},{4,0},{5,1},{6,2},{7,3},{8,12},{9,13},{10,... | collective-permute-start | bytes 786440 | tf_op jit(solution)/shard_map/ppermute | solution.py:326
  16.7 28.2 %collective-permute-start.5 = (bf16[1024,128]{1,0:T(8,128)(2,1)S(1)}, bf16[1024,128]{1,0:T(8,128)(2,1)S(1)}, u32[]{:S(2)}, u32[]{:S(2)}) collective-permute-start(bf16[1024,128]{1,0:T(8,128)(2,1)S(1)} %get-tuple-element.61), channel_id=1, source_target_pairs={{0,8},{1,9},{2,10},{3,11},{4,12},{5,13},{6,14},{7,15},{8,0},{9,1},... | collective-permute-start | bytes 786440 | tf_op jit(solution)/shard_map/ppermute | solution.py:326
  18.8 28.4 %collective-permute-start.6 = (bf16[1024,128]{1,0:T(8,128)(2,1)S(1)}, bf16[1024,128]{1,0:T(8,128)(2,1)S(1)}, u32[]{:S(2)}, u32[]{:S(2)}) collective-permute-start(bf16[1024,128]{1,0:T(8,128)(2,1)S(1)} %get-tuple-element.64), channel_id=1, source_target_pairs={{0,9},{1,8},{2,11},{3,10},{4,13},{5,12},{6,15},{7,14},{8,1},{9,0},... | collective-permute-start | bytes 786440 | tf_op jit(solution)/shard_map/ppermute | solution.py:326
  22.0 0.7 copy-start.17
  35.4 0.7 copy-start.7
  36.1 15.5 %collective-permute-start.1 = (bf16[1024,128]{1,0:T(8,128)(2,1)S(1)}, bf16[1024,128]{1,0:T(8,128)(2,1)S(1)}, u32[]{:S(2)}, u32[]{:S(2)}) collective-permute-start(bf16[1024,128]{1,0:T(8,128)(2,1)S(1)} %get-tuple-element.49), channel_id=1, source_target_pairs={{0,3},{1,2},{2,1},{3,0},{4,7},{5,6},{6,5},{7,4},{8,11},{9,10},{10,... | collective-permute-start | bytes 786440 | tf_op jit(solution)/shard_map/ppermute | solution.py:326
  38.6 0.7 copy-start.9
  39.3 28.9 %collective-permute-start.9 = (bf16[1024,128]{1,0:T(8,128)(2,1)S(1)}, bf16[1024,128]{1,0:T(8,128)(2,1)S(1)}, u32[]{:S(2)}, u32[]{:S(2)}) collective-permute-start(bf16[1024,128]{1,0:T(8,128)(2,1)S(1)} %get-tuple-element.73), channel_id=1, source_target_pairs={{0,2},{1,3},{2,0},{3,1},{4,6},{5,7},{6,4},{7,5},{8,10},{9,11},{10,... | collective-permute-start | bytes 786440 | tf_op jit(solution)/shard_map/ppermute | solution.py:326
  41.2 0.7 copy-start.11
  41.9 26.4 %collective-permute-start.10 = (bf16[1024,128]{1,0:T(8,128)(2,1)S(1)}, bf16[1024,128]{1,0:T(8,128)(2,1)S(1)}, u32[]{:S(2)}, u32[]{:S(2)}) collective-permute-start(bf16[1024,128]{1,0:T(8,128)(2,1)S(1)} %get-tuple-element.77), channel_id=1, source_target_pairs={{0,6},{1,7},{2,4},{3,5},{4,2},{5,3},{6,0},{7,1},{8,14},{9,15},{10,... | collective-permute-start | bytes 786440 | tf_op jit(solution)/shard_map/ppermute | solution.py:326
  44.9 0.7 copy-start.13
  45.6 29.1 %collective-permute-start.12 = (bf16[1024,128]{1,0:T(8,128)(2,1)S(1)}, bf16[1024,128]{1,0:T(8,128)(2,1)S(1)}, u32[]{:S(2)}, u32[]{:S(2)}) collective-permute-start(bf16[1024,128]{1,0:T(8,128)(2,1)S(1)} %get-tuple-element.80), channel_id=1, source_target_pairs={{0,10},{1,11},{2,8},{3,9},{4,14},{5,15},{6,12},{7,13},{8,2},{9,3},... | collective-permute-start | bytes 786440 | tf_op jit(solution)/shard_map/ppermute | solution.py:326
  47.2 0.7 copy-start.15
  47.9 48.8 %collective-permute-start.7 = (bf16[1024,128]{1,0:T(8,128)(2,1)}, bf16[1024,128]{1,0:T(8,128)(2,1)S(1)}, u32[]{:S(2)}, u32[]{:S(2)}) collective-permute-start(bf16[1024,128]{1,0:T(8,128)(2,1)} %get-tuple-element.70), channel_id=1, source_target_pairs={{0,11},{1,10},{2,9},{3,8},{4,15},{5,14},{6,13},{7,12},{8,3},{9,2},... | collective-permute-start | bytes 786440 | tf_op jit(solution)/shard_map/ppermute | solution.py:326
  51.6 69.3 %collective-permute-start.2 = (bf16[1024,128]{1,0:T(8,128)(2,1)S(1)}, bf16[1024,128]{1,0:T(8,128)(2,1)S(1)}, u32[]{:S(2)}, u32[]{:S(2)}) collective-permute-start(bf16[1024,128]{1,0:T(8,128)(2,1)S(1)} %get-tuple-element.50), channel_id=1, source_target_pairs={{0,14},{1,15},{2,12},{3,13},{4,10},{5,11},{6,8},{7,9},{8,6},{9,7},... | collective-permute-start | bytes 786440 | tf_op jit(solution)/shard_map/ppermute | solution.py:326
  68.2 40.3 %collective-permute-start.11 = (bf16[1024,128]{1,0:T(8,128)(2,1)}, bf16[1024,128]{1,0:T(8,128)(2,1)S(1)}, u32[]{:S(2)}, u32[]{:S(2)}) collective-permute-start(bf16[1024,128]{1,0:T(8,128)(2,1)} %get-tuple-element.78), channel_id=1, source_target_pairs={{0,12},{1,13},{2,14},{3,15},{4,8},{5,9},{6,10},{7,11},{8,4},{9,5},... | collective-permute-start | bytes 786440 | tf_op jit(solution)/shard_map/ppermute | solution.py:326
  74.7 40.1 %collective-permute-start.13 = (bf16[1024,128]{1,0:T(8,128)(2,1)}, bf16[1024,128]{1,0:T(8,128)(2,1)S(1)}, u32[]{:S(2)}, u32[]{:S(2)}) collective-permute-start(bf16[1024,128]{1,0:T(8,128)(2,1)} %get-tuple-element.81), channel_id=1, source_target_pairs={{0,13},{1,12},{2,15},{3,14},{4,9},{5,8},{6,11},{7,10},{8,5},{9,4},... | collective-permute-start | bytes 786440 | tf_op jit(solution)/shard_map/ppermute | solution.py:326
  77.1 23.1 %collective-permute-start.14 = (bf16[1024,128]{1,0:T(8,128)(2,1)}, bf16[1024,128]{1,0:T(8,128)(2,1)S(1)}, u32[]{:S(2)}, u32[]{:S(2)}) collective-permute-start(bf16[1024,128]{1,0:T(8,128)(2,1)} %get-tuple-element.83), channel_id=1, source_target_pairs={{0,7},{1,6},{2,5},{3,4},{4,3},{5,2},{6,1},{7,0},{8,15},{9,14},{10,... | collective-permute-start | bytes 786440 | tf_op jit(solution)/shard_map/ppermute | solution.py:326
  81.8 1.0 copy-start.8
  82.8 0.9 copy-start.10
  83.8 0.9 copy-start.12
  84.7 0.9 copy-start.14
  85.7 0.9 copy-start.16
  86.6 0.9 copy-start.18
  96.7 24.2 %collective-permute-start.8 = (bf16[1024,128]{1,0:T(8,128)(2,1)S(1)}, bf16[1024,128]{1,0:T(8,128)(2,1)S(1)}, u32[]{:S(2)}, u32[]{:S(2)}) collective-permute-start(bf16[1024,128]{1,0:T(8,128)(2,1)S(1)} %get-tuple-element.71), channel_id=1, source_target_pairs={{0,15},{1,14},{2,13},{3,12},{4,11},{5,10},{6,9},{7,8},{8,7},{9,6},... | collective-permute-start | bytes 786440 | tf_op jit(solution)/shard_map/ppermute | solution.py:326
  (3 other events, 2.0 us)

commit v3 on v2

--- a/solution.py
+++ b/solution.py
@@ -12,7 +12,7 @@
 UNIT_ROWS = 16
 B_BLOCK = 64
 ACC = jnp.bfloat16
-GROUPS = ((0, 2, 4), (3, 5), (1, 6), (7,))
+GROUPS = ((0, 2, 4), (1, 3, 5), (6,), (7,))
 IN_FLIGHT = 5
 FAR_TURNS = (2, 4)
 SMALL_VMEM = 16 * 1024 * 1024

time: 128 us -> 128 us (level)
  local copies, waits for them, and re-layouts: 15 us -> 11.2 us
  starting transfers between devices: 31.5 us -> 32.9 us
  waiting for transfers between devices: 46.1 us -> 47.4 us
    unnamed x38, local copies, waits for them, and re-layouts: 15 us -> 11.2 us
    ppermute x15, starting transfers between devices: 24.9 us -> 26.3 us  [send(): lax.ppermute(piece, 'work', [(i, i ^ shift) for i in range(workers)])]
    ppermute x15, waiting for transfers between devices: 46.1 us -> 47.4 us  [send(): lax.ppermute(piece, 'work', [(i, i ^ shift) for i in range(workers)])]
  transfers between devices with their start and end apart: 16 -> 16, of which waited for: 7 -> 8; matrix products, arithmetic and copies ran while one was open for 0% -> 0% of each run, Pallas kernels for 20% -> 21%
where the time goes in v3:
time: 128 us; the launch traced here: 127 us
  waiting for transfers between devices  47.4 us (37%)
  Pallas kernels  35.6 us (28%)
  starting transfers between devices  32.9 us (26%)
  local copies, waits for them, and re-layouts  11.2 us (9%)
    ppermute x15, waiting for transfers between devices, send(): lax.ppermute(piece, 'work', [(i, i ^ shift) for i in range(workers)])  47.4 us
    pallas_call x4, Pallas kernels, add_group(): pl.pallas_call(functools.partial(group_kernel, first, last, units, per_un...  29 us
    ppermute x15, starting transfers between devices, send(): lax.ppermute(piece, 'work', [(i, i ^ shift) for i in range(workers)])  26.3 us
    unnamed x38, local copies, waits for them, and re-layouts  11.2 us
    all_to_all x1, starting transfers between devices, per_device(): lax.all_to_all(matrices, 'work', split_axis=0, concat_axis=0, tiled=True)  6.61 us
    pallas_call x2, Pallas kernels, choose_pieces(): pl.pallas_call(functools.partial(pieces_kernel, shifts), in_specs=[pl.Blo...  2.75 us
  transfers between devices with their start and end apart: 16, of which 8 were waited for; matrix products, arithmetic and copies ran while one was open for 0% of the time, Pallas kernels for 21%

profile of v3, /device:TPU:11, one launch (start us, length us, event | category | flops | bytes accessed | tf_op | source)
XLA Modules:
  0.0 127.5 jit_solution(3386448504479020023)
XLA Ops:
  0.0 0.9 copy-done.1
  2.3 2.2 %shard_map.66 = bf16[16,144,128]{2,1,0:T(8,128)(2,1)} custom-call(s32[16]{0:T(128)S(1)} %copy-done.4, s32[3,48]{1,0:T(4,128)S(1)} %bitcast.2, bf16[96,1024]{1,0:T(8,128)(2,1)S(1)} %copy-done.1), custom_call_target="tpu_custom_call" | custom-call | tf_op jit(solution)/shard_map/pallas_call | solution.py:89
  4.5 6.6 %all-to-all-start = ((bf16[16,144,128]{2,1,0:T(8,128)(2,1)}), bf16[16,144,128]{2,1,0:T(8,128)(2,1)S(1)}, u32[]{:S(2)}, u32[]{:S(2)}) async-start(bf16[16,144,128]{2,1,0:T(8,128)(2,1)} %shard_map.66), calls=%async_computation | async-start | bytes 1179648 | tf_op jit(solution)/shard_map/all_to_all | solution.py:331
  11.1 2.2 %copy-done = bf16[16,1024,128]{2,1,0:T(8,128)(2,1)S(1)} copy-done((bf16[16,1024,128]{2,1,0:T(8,128)(2,1)S(1)}, bf16[16,1024,128]{2,1,0:T(8,128)(2,1)}, u32[]{:S(2)}) %copy-start) | copy-done | bytes 4194328
  13.9 0.9 shard_map.65
  14.9 1.6 %collective-permute-start.4 = (bf16[1024,128]{1,0:T(8,128)(2,1)S(1)}, bf16[1024,128]{1,0:T(8,128)(2,1)S(1)}, u32[]{:S(2)}, u32[]{:S(2)}) collective-permute-start(bf16[1024,128]{1,0:T(8,128)(2,1)S(1)} %get-tuple-element.57), channel_id=1, source_target_pairs={{0,4},{1,5},{2,6},{3,7},{4,0},{5,1},{6,2},{7,3},{8,12},{9,13},{10,... | collective-permute-start | bytes 786440 | tf_op jit(solution)/shard_map/ppermute | solution.py:326
  16.6 2.1 %collective-permute-start.5 = (bf16[1024,128]{1,0:T(8,128)(2,1)S(1)}, bf16[1024,128]{1,0:T(8,128)(2,1)S(1)}, u32[]{:S(2)}, u32[]{:S(2)}) collective-permute-start(bf16[1024,128]{1,0:T(8,128)(2,1)S(1)} %get-tuple-element.61), channel_id=1, source_target_pairs={{0,8},{1,9},{2,10},{3,11},{4,12},{5,13},{6,14},{7,15},{8,0},{9,1},... | collective-permute-start | bytes 786440 | tf_op jit(solution)/shard_map/ppermute | solution.py:326
  18.7 0.7 collective-permute-start.3
  19.6 1.9 %shard_map.64 = (bf16[1024,128]{1,0:T(8,128)(2,1)S(1)}, bf16[1024,128]{1,0:T(8,128)(2,1)S(1)}, bf16[1024,128]{1,0:T(8,128)(2,1)S(1)}, bf16[1024,128]{1,0:T(8,128...) custom-call(s32[16]{0:T(128)S(1)} %copy-done.3, ...), custom_call_target="tpu_custom_call" | custom-call | tf_op jit(solution)/shard_map/pallas_call | solution.py:42
  22.2 13.2 %collective-permute-done.refs_3_ = bf16[1024,128]{1,0:T(8,128)(2,1)S(1)} collective-permute-done((bf16[1024,128]{1,0:T(8,128)(2,1)S(1)}, bf16[1024,128]{1,0:T(8,128)(2,1)S(1)}, u32[]{:S(2)}, u32[]{:S(2)}) %collective-permute-start) | collective-permute-done | bytes 262176 | tf_op jit(solution)/shard_map/ppermute | solution.py:326
  35.4 2.5 %collective-permute-start.1 = (bf16[1024,128]{1,0:T(8,128)(2,1)S(1)}, bf16[1024,128]{1,0:T(8,128)(2,1)S(1)}, u32[]{:S(2)}, u32[]{:S(2)}) collective-permute-start(bf16[1024,128]{1,0:T(8,128)(2,1)S(1)} %get-tuple-element.49), channel_id=1, source_target_pairs={{0,3},{1,2},{2,1},{3,0},{4,7},{5,6},{6,5},{7,4},{8,11},{9,10},{10,... | collective-permute-start | bytes 786440 | tf_op jit(solution)/shard_map/ppermute | solution.py:326
  37.9 3.2 %collective-permute-done.4.refs_2_ = bf16[1024,128]{1,0:T(8,128)(2,1)S(1)} collective-permute-done((bf16[1024,128]{1,0:T(8,128)(2,1)S(1)}, bf16[1024,128]{1,0:T(8,128)(2,1)S(1)}, u32[]{:S(2)}, u32[]{:S(2)}) %collective-permute-start.4) | collective-permute-done | bytes 262176 | tf_op jit(solution)/shard_map/ppermute | solution.py:326
  41.2 3.1 %collective-permute-start.9 = (bf16[1024,128]{1,0:T(8,128)(2,1)S(1)}, bf16[1024,128]{1,0:T(8,128)(2,1)S(1)}, u32[]{:S(2)}, u32[]{:S(2)}) collective-permute-start(bf16[1024,128]{1,0:T(8,128)(2,1)S(1)} %get-tuple-element.73), channel_id=1, source_target_pairs={{0,6},{1,7},{2,4},{3,5},{4,2},{5,3},{6,0},{7,1},{8,14},{9,15},{10,... | collective-permute-start | bytes 786440 | tf_op jit(solution)/shard_map/ppermute | solution.py:326
  44.7 2.5 %collective-permute-done.6.refs_5_ = bf16[1024,128]{1,0:T(8,128)(2,1)S(1)} collective-permute-done((bf16[1024,128]{1,0:T(8,128)(2,1)S(1)}, bf16[1024,128]{1,0:T(8,128)(2,1)S(1)}, u32[]{:S(2)}, u32[]{:S(2)}) %collective-permute-start.6) | collective-permute-done | bytes 262176 | tf_op jit(solution)/shard_map/ppermute | solution.py:326
  47.2 0.7 copy-done.7
  47.9 3.6 %collective-permute-start.7 = (bf16[1024,128]{1,0:T(8,128)(2,1)}, bf16[1024,128]{1,0:T(8,128)(2,1)}, u32[]{:S(2)}, u32[]{:S(2)}) collective-permute-start(bf16[1024,128]{1,0:T(8,128)(2,1)} %get-tuple-element.70), channel_id=1, source_target_pairs={{0,11},{1,10},{2,9},{3,8},{4,15},{5,14},{6,13},{7,12},{8,3},{9,2},... | collective-permute-start | bytes 786440 | tf_op jit(solution)/shard_map/ppermute | solution.py:326
  52.3 1.2 collective-permute-start.2
  53.5 2.0 %collective-permute-done.9.refs_2_ = bf16[1024,128]{1,0:T(8,128)(2,1)S(1)} collective-permute-done((bf16[1024,128]{1,0:T(8,128)(2,1)S(1)}, bf16[1024,128]{1,0:T(8,128)(2,1)S(1)}, u32[]{:S(2)}, u32[]{:S(2)}) %collective-permute-start.9) | collective-permute-done | bytes 262176 | tf_op jit(solution)/shard_map/ppermute | solution.py:326
  56.2 1.7 %collective-permute-start.10 = (bf16[1024,128]{1,0:T(8,128)(2,1)S(1)}, bf16[1024,128]{1,0:T(8,128)(2,1)S(1)}, u32[]{:S(2)}, u32[]{:S(2)}) collective-permute-start(bf16[1024,128]{1,0:T(8,128)(2,1)S(1)} %get-tuple-element.74), channel_id=1, source_target_pairs={{0,12},{1,13},{2,14},{3,15},{4,8},{5,9},{6,10},{7,11},{8,4},{9,5},... | collective-permute-start | bytes 786440 | tf_op jit(solution)/shard_map/ppermute | solution.py:326
  57.9 16.8 %collective-permute-done.11.refs_4_ = bf16[1024,128]{1,0:T(8,128)(2,1)S(1)} collective-permute-done((bf16[1024,128]{1,0:T(8,128)(2,1)S(1)}, bf16[1024,128]{1,0:T(8,128)(2,1)S(1)}, u32[]{:S(2)}, u32[]{:S(2)}) %collective-permute-start.11) | collective-permute-done | bytes 262176 | tf_op jit(solution)/shard_map/ppermute | solution.py:326
  75.4 2.4 %collective-permute-start.12 = (bf16[1024,128]{1,0:T(8,128)(2,1)S(1)}, bf16[1024,128]{1,0:T(8,128)(2,1)S(1)}, u32[]{:S(2)}, u32[]{:S(2)}) collective-permute-start(bf16[1024,128]{1,0:T(8,128)(2,1)S(1)} %get-tuple-element.77), channel_id=1, source_target_pairs={{0,13},{1,12},{2,15},{3,14},{4,9},{5,8},{6,11},{7,10},{8,5},{9,4},... | collective-permute-start | bytes 786440 | tf_op jit(solution)/shard_map/ppermute | solution.py:326
  78.5 3.0 %collective-permute-start.14 = (bf16[1024,128]{1,0:T(8,128)(2,1)}, bf16[1024,128]{1,0:T(8,128)(2,1)}, u32[]{:S(2)}, u32[]{:S(2)}) collective-permute-start(bf16[1024,128]{1,0:T(8,128)(2,1)} %get-tuple-element.83), channel_id=1, source_target_pairs={{0,7},{1,6},{2,5},{3,4},{4,3},{5,2},{6,1},{7,0},{8,15},{9,14},{10,... | collective-permute-start | bytes 786440 | tf_op jit(solution)/shard_map/ppermute | solution.py:326
  81.6 1.7 %shard_map.67 = (bf16[128,768]{1,0:T(8,128)(2,1)S(1)}, bf16[768,128]{1,0:T(8,128)(2,1)S(1)}, bf16[8,96,128]{2,1,0:T(8,128)(2,1)S(1)}) custom-call(s32[16]{0:T(128)S(1)} %copy-done.5, f32[48]{0:T(128)S(1)} %copy-done.6, bf16[16,144,128]{2,1,0:T(8,128)(2,1)S(1)} %all-to-all-done.matrix_ref), custom_call_target="tpu_custom_call" | custom-call | tf_op jit(solution)/shard_map/pallas_call | solution.py:145
  83.3 0.9 copy-done.8
  84.2 0.9 copy-done.10
  85.2 9.2 %shard_map.68.refs_9_ = bf16[128,128,128]{2,1,0:T(8,128)(2,1)S(1)} custom-call(bf16[1024,128]{1,0:T(8,128)(2,1)S(1)} %copy-done.10, bf16[1024,128]{1,0:T(8,128)(2,1)S(1)} %collective-permute-done.3.refs_1_, bf16[1024,128]{1,0:T(8,128)(2,1)S(1)} %collective-permute-done.4.refs_2_, bf16[1024,128]{1,0:T(8,128)(2,1)S(1)} %collective-permute-done.refs_3_, ...), custom_call_target="tpu_custom_call" | custom-call | flops 3623878656 | bytes 25165824 | tf_op jit(solution)/shard_map/pallas_call | solution.py:285
  94.4 3.5 %collective-permute-start.8 = (bf16[1024,128]{1,0:T(8,128)(2,1)S(1)}, bf16[1024,128]{1,0:T(8,128)(2,1)S(1)}, u32[]{:S(2)}, u32[]{:S(2)}) collective-permute-start(bf16[1024,128]{1,0:T(8,128)(2,1)S(1)} %get-tuple-element.71), channel_id=1, source_target_pairs={{0,15},{1,14},{2,13},{3,12},{4,11},{5,10},{6,9},{7,8},{8,7},{9,6},... | collective-permute-start | bytes 786440 | tf_op jit(solution)/shard_map/ppermute | solution.py:326
  97.9 9.8 %shard_map.69.refs_5_ = bf16[128,128,128]{2,1,0:T(8,128)(2,1)S(1)} custom-call(bf16[1024,128]{1,0:T(8,128)(2,1)S(1)} %copy-done.18, bf16[1024,128]{1,0:T(8,128)(2,1)S(1)} %copy-done.12, bf16[1024,128]{1,0:T(8,128)(2,1)S(1)} %copy-done.14, bf16[1024,128]{1,0:T(8,128)(2,1)} %collective-permute-done.14.refs_3_, bf16[1024,128]{1,0:T(8,128)(2,1)S(1)} %copy-done.16, ...), custom_call_target="tpu_custom_call" | custom-call | flops 3623878656 | bytes 25165824 | tf_op jit(solution)/shard_map/pallas_call | solution.py:285
  108.1 6.3 %collective-permute-done.12.refs_1_ = bf16[1024,128]{1,0:T(8,128)(2,1)S(1)} collective-permute-done((bf16[1024,128]{1,0:T(8,128)(2,1)S(1)}, bf16[1024,128]{1,0:T(8,128)(2,1)S(1)}, u32[]{:S(2)}, u32[]{:S(2)}) %collective-permute-start.12) | collective-permute-done | bytes 262176 | tf_op jit(solution)/shard_map/ppermute | solution.py:326
  114.3 3.8 %shard_map.70.refs_5_ = bf16[128,128,128]{2,1,0:T(8,128)(2,1)S(1)} custom-call(bf16[1024,128]{1,0:T(8,128)(2,1)S(1)} %collective-permute-done.10.refs_0_, bf16[1024,128]{1,0:T(8,128)(2,1)S(1)} %collective-permute-done.12.refs_1_, bf16[128,768]{1,0:T(8,128)(2,1)S(1)} %get-tuple-element.66.refs_6_.refs_2_, ...), custom_call_target="tpu_custom_call" | custom-call | flops 1207959552 | bytes 25165824 | tf_op jit(solution)/shard_map/pallas_call | solution.py:285
  118.2 2.9 %collective-permute-done.8.refs_1_ = bf16[1024,128]{1,0:T(8,128)(2,1)S(1)} collective-permute-done((bf16[1024,128]{1,0:T(8,128)(2,1)S(1)}, bf16[1024,128]{1,0:T(8,128)(2,1)S(1)}, u32[]{:S(2)}, u32[]{:S(2)}) %collective-permute-start.8) | collective-permute-done | bytes 262176 | tf_op jit(solution)/shard_map/ppermute | solution.py:326
  121.1 6.2 %shard_map.71 = bf16[128,128,128]{2,1,0:T(8,128)(2,1)} custom-call(bf16[1024,128]{1,0:T(8,128)(2,1)S(1)} %collective-permute-done.2.refs_0_, bf16[1024,128]{1,0:T(8,128)(2,1)S(1)} %collective-permute-done.8.refs_1_, bf16[128,768]{1,0:T(8,128)(2,1)S(1)} %get-tuple-element.66.refs_6_.refs_2_, bf16[768,128]{1,0:T(8,128)(2,1)S(1)} %get-tuple-element.67.refs_7_.refs_3_, ...), custom_call_target="tpu_custom_call" | custom-call | flops 1207959552 | bytes 25165824 | tf_op jit(solution)/shard_map/pallas_call | solution.py:285
  (46 shorter events, 6.8 us)
Async XLA Ops:
  0.0 0.9 copy-start.1
  4.5 77.1 %all-to-all-start = ((bf16[16,144,128]{2,1,0:T(8,128)(2,1)}), bf16[16,144,128]{2,1,0:T(8,128)(2,1)S(1)}, u32[]{:S(2)}, u32[]{:S(2)}) async-start(bf16[16,144,128]{2,1,0:T(8,128)(2,1)} %shard_map.66), calls=%async_computation | async-start | bytes 1179648 | tf_op jit(solution)/shard_map/all_to_all | solution.py:331
  11.1 2.2 %copy-start = (bf16[16,1024,128]{2,1,0:T(8,128)(2,1)S(1)}, bf16[16,1024,128]{2,1,0:T(8,128)(2,1)}, u32[]{:S(2)}) copy-start(bf16[16,1024,128]{2,1,0:T(8,128)(2,1)} %source_ref.3) | copy-start | bytes 12582916
  13.9 67.6 %copy-start.5 = (s32[16]{0:T(128)S(1)}, s32[16]{0:T(128)}, u32[]{:S(2)}) copy-start(s32[16]{0:T(128)} %counts_ref.3) | copy-start | bytes 196
  13.9 67.6 %copy-start.6 = (f32[48]{0:T(128)S(1)}, f32[48]{0:T(128)}, u32[]{:S(2)}) copy-start(f32[48]{0:T(128)} %weights_ref.1) | copy-start | bytes 580
  14.8 20.6 %collective-permute-start = (bf16[1024,128]{1,0:T(8,128)(2,1)S(1)}, bf16[1024,128]{1,0:T(8,128)(2,1)S(1)}, u32[]{:S(2)}, u32[]{:S(2)}) collective-permute-start(bf16[1024,128]{1,0:T(8,128)(2,1)S(1)} %get-tuple-element.48), channel_id=1, source_target_pairs={{0,5},{1,4},{2,7},{3,6},{4,1},{5,0},{6,3},{7,2},{8,13},{9,12},{10,... | collective-permute-start | bytes 786440 | tf_op jit(solution)/shard_map/ppermute | solution.py:326
  14.9 26.2 %collective-permute-start.4 = (bf16[1024,128]{1,0:T(8,128)(2,1)S(1)}, bf16[1024,128]{1,0:T(8,128)(2,1)S(1)}, u32[]{:S(2)}, u32[]{:S(2)}) collective-permute-start(bf16[1024,128]{1,0:T(8,128)(2,1)S(1)} %get-tuple-element.57), channel_id=1, source_target_pairs={{0,4},{1,5},{2,6},{3,7},{4,0},{5,1},{6,2},{7,3},{8,12},{9,13},{10,... | collective-permute-start | bytes 786440 | tf_op jit(solution)/shard_map/ppermute | solution.py:326
  16.6 27.6 %collective-permute-start.5 = (bf16[1024,128]{1,0:T(8,128)(2,1)S(1)}, bf16[1024,128]{1,0:T(8,128)(2,1)S(1)}, u32[]{:S(2)}, u32[]{:S(2)}) collective-permute-start(bf16[1024,128]{1,0:T(8,128)(2,1)S(1)} %get-tuple-element.61), channel_id=1, source_target_pairs={{0,8},{1,9},{2,10},{3,11},{4,12},{5,13},{6,14},{7,15},{8,0},{9,1},... | collective-permute-start | bytes 786440 | tf_op jit(solution)/shard_map/ppermute | solution.py:326
  18.7 25.6 %collective-permute-start.3 = (bf16[1024,128]{1,0:T(8,128)(2,1)S(1)}, bf16[1024,128]{1,0:T(8,128)(2,1)S(1)}, u32[]{:S(2)}, u32[]{:S(2)}) collective-permute-start(bf16[1024,128]{1,0:T(8,128)(2,1)S(1)} %get-tuple-element.54), channel_id=1, source_target_pairs={{0,1},{1,0},{2,3},{3,2},{4,5},{5,4},{6,7},{7,6},{8,9},{9,8},{10,11... | collective-permute-start | bytes 786440 | tf_op jit(solution)/shard_map/ppermute | solution.py:326
  19.4 27.8 %collective-permute-start.6 = (bf16[1024,128]{1,0:T(8,128)(2,1)S(1)}, bf16[1024,128]{1,0:T(8,128)(2,1)S(1)}, u32[]{:S(2)}, u32[]{:S(2)}) collective-permute-start(bf16[1024,128]{1,0:T(8,128)(2,1)S(1)} %get-tuple-element.64), channel_id=1, source_target_pairs={{0,9},{1,8},{2,11},{3,10},{4,13},{5,12},{6,15},{7,14},{8,1},{9,0},... | collective-permute-start | bytes 786440 | tf_op jit(solution)/shard_map/ppermute | solution.py:326
  21.5 0.7 copy-start.9
  35.4 16.2 %collective-permute-start.1 = (bf16[1024,128]{1,0:T(8,128)(2,1)S(1)}, bf16[1024,128]{1,0:T(8,128)(2,1)S(1)}, u32[]{:S(2)}, u32[]{:S(2)}) collective-permute-start(bf16[1024,128]{1,0:T(8,128)(2,1)S(1)} %get-tuple-element.49), channel_id=1, source_target_pairs={{0,3},{1,2},{2,1},{3,0},{4,7},{5,6},{6,5},{7,4},{8,11},{9,10},{10,... | collective-permute-start | bytes 786440 | tf_op jit(solution)/shard_map/ppermute | solution.py:326
  41.2 14.4 %collective-permute-start.9 = (bf16[1024,128]{1,0:T(8,128)(2,1)S(1)}, bf16[1024,128]{1,0:T(8,128)(2,1)S(1)}, u32[]{:S(2)}, u32[]{:S(2)}) collective-permute-start(bf16[1024,128]{1,0:T(8,128)(2,1)S(1)} %get-tuple-element.73), channel_id=1, source_target_pairs={{0,6},{1,7},{2,4},{3,5},{4,2},{5,3},{6,0},{7,1},{8,14},{9,15},{10,... | collective-permute-start | bytes 786440 | tf_op jit(solution)/shard_map/ppermute | solution.py:326
  44.2 30.5 %collective-permute-start.11 = (bf16[1024,128]{1,0:T(8,128)(2,1)S(1)}, bf16[1024,128]{1,0:T(8,128)(2,1)S(1)}, u32[]{:S(2)}, u32[]{:S(2)}) collective-permute-start(bf16[1024,128]{1,0:T(8,128)(2,1)S(1)} %get-tuple-element.76), channel_id=1, source_target_pairs={{0,10},{1,11},{2,8},{3,9},{4,14},{5,15},{6,12},{7,13},{8,2},{9,3},... | collective-permute-start | bytes 786440 | tf_op jit(solution)/shard_map/ppermute | solution.py:326
  44.3 33.5 %collective-permute-start.13 = (bf16[1024,128]{1,0:T(8,128)(2,1)S(1)}, bf16[1024,128]{1,0:T(8,128)(2,1)S(1)}, u32[]{:S(2)}, u32[]{:S(2)}) collective-permute-start(bf16[1024,128]{1,0:T(8,128)(2,1)S(1)} %get-tuple-element.79), channel_id=1, source_target_pairs={{0,2},{1,3},{2,0},{3,1},{4,6},{5,7},{6,4},{7,5},{8,10},{9,11},{10,... | collective-permute-start | bytes 786440 | tf_op jit(solution)/shard_map/ppermute | solution.py:326
  47.2 0.7 copy-start.7
  47.9 46.4 %collective-permute-start.7 = (bf16[1024,128]{1,0:T(8,128)(2,1)}, bf16[1024,128]{1,0:T(8,128)(2,1)}, u32[]{:S(2)}, u32[]{:S(2)}) collective-permute-start(bf16[1024,128]{1,0:T(8,128)(2,1)} %get-tuple-element.70), channel_id=1, source_target_pairs={{0,11},{1,10},{2,9},{3,8},{4,15},{5,14},{6,13},{7,12},{8,3},{9,2},... | collective-permute-start | bytes 786440 | tf_op jit(solution)/shard_map/ppermute | solution.py:326
  51.6 0.7 copy-start.11
  52.3 65.9 %collective-permute-start.2 = (bf16[1024,128]{1,0:T(8,128)(2,1)S(1)}, bf16[1024,128]{1,0:T(8,128)(2,1)S(1)}, u32[]{:S(2)}, u32[]{:S(2)}) collective-permute-start(bf16[1024,128]{1,0:T(8,128)(2,1)S(1)} %get-tuple-element.50), channel_id=1, source_target_pairs={{0,14},{1,15},{2,12},{3,13},{4,10},{5,11},{6,8},{7,9},{8,6},{9,7},... | collective-permute-start | bytes 786440 | tf_op jit(solution)/shard_map/ppermute | solution.py:326
  55.5 0.7 copy-start.13
  56.2 51.8 %collective-permute-start.10 = (bf16[1024,128]{1,0:T(8,128)(2,1)S(1)}, bf16[1024,128]{1,0:T(8,128)(2,1)S(1)}, u32[]{:S(2)}, u32[]{:S(2)}) collective-permute-start(bf16[1024,128]{1,0:T(8,128)(2,1)S(1)} %get-tuple-element.74), channel_id=1, source_target_pairs={{0,12},{1,13},{2,14},{3,15},{4,8},{5,9},{6,10},{7,11},{8,4},{9,5},... | collective-permute-start | bytes 786440 | tf_op jit(solution)/shard_map/ppermute | solution.py:326
  74.7 0.7 copy-start.15
  75.4 39.0 %collective-permute-start.12 = (bf16[1024,128]{1,0:T(8,128)(2,1)S(1)}, bf16[1024,128]{1,0:T(8,128)(2,1)S(1)}, u32[]{:S(2)}, u32[]{:S(2)}) collective-permute-start(bf16[1024,128]{1,0:T(8,128)(2,1)S(1)} %get-tuple-element.77), channel_id=1, source_target_pairs={{0,13},{1,12},{2,15},{3,14},{4,9},{5,8},{6,11},{7,10},{8,5},{9,4},... | collective-permute-start | bytes 786440 | tf_op jit(solution)/shard_map/ppermute | solution.py:326
  77.8 0.7 copy-start.17
  78.5 19.4 %collective-permute-start.14 = (bf16[1024,128]{1,0:T(8,128)(2,1)}, bf16[1024,128]{1,0:T(8,128)(2,1)}, u32[]{:S(2)}, u32[]{:S(2)}) collective-permute-start(bf16[1024,128]{1,0:T(8,128)(2,1)} %get-tuple-element.83), channel_id=1, source_target_pairs={{0,7},{1,6},{2,5},{3,4},{4,3},{5,2},{6,1},{7,0},{8,15},{9,14},{10,... | collective-permute-start | bytes 786440 | tf_op jit(solution)/shard_map/ppermute | solution.py:326
  83.3 1.0 copy-start.8
  84.2 0.9 copy-start.10
  85.2 12.7 %copy-start.12 = (bf16[1024,128]{1,0:T(8,128)(2,1)S(1)}, bf16[1024,128]{1,0:T(8,128)(2,1)}, u32[]{:S(2)}) copy-start(bf16[1024,128]{1,0:T(8,128)(2,1)} %copy-done.11) | copy-start | bytes 786436
  85.2 12.7 %copy-start.14 = (bf16[1024,128]{1,0:T(8,128)(2,1)S(1)}, bf16[1024,128]{1,0:T(8,128)(2,1)}, u32[]{:S(2)}) copy-start(bf16[1024,128]{1,0:T(8,128)(2,1)} %copy-done.13) | copy-start | bytes 786436
  85.2 12.7 %copy-start.16 = (bf16[1024,128]{1,0:T(8,128)(2,1)S(1)}, bf16[1024,128]{1,0:T(8,128)(2,1)}, u32[]{:S(2)}) copy-start(bf16[1024,128]{1,0:T(8,128)(2,1)} %copy-done.15) | copy-start | bytes 786436
  85.2 12.7 %copy-start.18 = (bf16[1024,128]{1,0:T(8,128)(2,1)S(1)}, bf16[1024,128]{1,0:T(8,128)(2,1)}, u32[]{:S(2)}) copy-start(bf16[1024,128]{1,0:T(8,128)(2,1)} %copy-done.17) | copy-start | bytes 786436
  94.4 26.7 %collective-permute-start.8 = (bf16[1024,128]{1,0:T(8,128)(2,1)S(1)}, bf16[1024,128]{1,0:T(8,128)(2,1)S(1)}, u32[]{:S(2)}, u32[]{:S(2)}) collective-permute-start(bf16[1024,128]{1,0:T(8,128)(2,1)S(1)} %get-tuple-element.71), channel_id=1, source_target_pairs={{0,15},{1,14},{2,13},{3,12},{4,11},{5,10},{6,9},{7,8},{8,7},{9,6},... | collective-permute-start | bytes 786440 | tf_op jit(solution)/shard_map/ppermute | solution.py:326
  (3 other events, 2.0 us)

commit v4 on v3

--- a/solution.py
+++ b/solution.py
@@ -331,6 +331,9 @@
     matrices = lax.all_to_all(matrices, "work", split_axis=0, concat_axis=0, tiled=True)
     leg3, leg2, leg1 = make_legs(matrices, sink_counts, weights, workers)
     for place in range(IN_FLIGHT, len(order) - 1):
+        if place == 2 * IN_FLIGHT:
+            shift = order[place]
+            pieces[shift], leg3 = lax.optimization_barrier((pieces[shift], leg3))
         send(place)
 
     acc = None

time: 128 us -> 128 us (level)
    unnamed x38 -> x36, local copies, waits for them, and re-layouts: 11.2 us -> 11.2 us
  transfers between devices with their start and end apart: 16 -> 16, of which waited for: 8 -> 7; matrix products, arithmetic and copies ran while one was open for 0% -> 0% of each run, Pallas kernels for 21% -> 22%
where the time goes in v4:
time: 128 us
  waiting for transfers between devices  46.3 us (36%)
  Pallas kernels  36.7 us (29%)
  starting transfers between devices  33 us (26%)
  local copies, waits for them, and re-layouts  11.2 us (9%)
    ppermute x15, waiting for transfers between devices, send(): lax.ppermute(piece, 'work', [(i, i ^ shift) for i in range(workers)])  46.3 us
    pallas_call x4, Pallas kernels, add_group(): pl.pallas_call(functools.partial(group_kernel, first, last, units, per_un...  30.1 us
    ppermute x15, starting transfers between devices, send(): lax.ppermute(piece, 'work', [(i, i ^ shift) for i in range(workers)])  26.4 us
    unnamed x36, local copies, waits for them, and re-layouts  11.2 us
    all_to_all x1, starting transfers between devices, per_device(): lax.all_to_all(matrices, 'work', split_axis=0, concat_axis=0, tiled=True)  6.61 us
    pallas_call x2, Pallas kernels, choose_pieces(): pl.pallas_call(functools.partial(pieces_kernel, shifts), in_specs=[pl.Blo...  2.67 us
  transfers between devices with their start and end apart: 16, of which 7 were waited for; matrix products, arithmetic and copies ran while one was open for 0% of the time, Pallas kernels for 22%

profile of v4, /device:TPU:11, one launch (start us, length us, event | category | flops | bytes accessed | tf_op | source)
XLA Modules:
  0.0 127.6 jit_solution(15335685926686777246)
XLA Ops:
  0.0 0.9 copy-done.1
  2.3 2.2 %shard_map.66 = bf16[16,144,128]{2,1,0:T(8,128)(2,1)} custom-call(s32[16]{0:T(128)S(1)} %copy-done.4, s32[3,48]{1,0:T(4,128)S(1)} %bitcast.2, bf16[96,1024]{1,0:T(8,128)(2,1)S(1)} %copy-done.1), custom_call_target="tpu_custom_call" | custom-call | tf_op jit(solution)/shard_map/pallas_call | solution.py:89
  4.5 6.6 %all-to-all-start = ((bf16[16,144,128]{2,1,0:T(8,128)(2,1)}), bf16[16,144,128]{2,1,0:T(8,128)(2,1)S(1)}, u32[]{:S(2)}, u32[]{:S(2)}) async-start(bf16[16,144,128]{2,1,0:T(8,128)(2,1)} %shard_map.66), calls=%async_computation | async-start | bytes 1179648 | tf_op jit(solution)/shard_map/all_to_all | solution.py:331
  11.1 2.2 %copy-done = bf16[16,1024,128]{2,1,0:T(8,128)(2,1)S(1)} copy-done((bf16[16,1024,128]{2,1,0:T(8,128)(2,1)S(1)}, bf16[16,1024,128]{2,1,0:T(8,128)(2,1)}, u32[]{:S(2)}) %copy-start) | copy-done | bytes 4194328
  13.9 0.9 shard_map.65
  14.9 1.6 %collective-permute-start.4 = (bf16[1024,128]{1,0:T(8,128)(2,1)S(1)}, bf16[1024,128]{1,0:T(8,128)(2,1)S(1)}, u32[]{:S(2)}, u32[]{:S(2)}) collective-permute-start(bf16[1024,128]{1,0:T(8,128)(2,1)S(1)} %get-tuple-element.59), channel_id=1, source_target_pairs={{0,4},{1,5},{2,6},{3,7},{4,0},{5,1},{6,2},{7,3},{8,12},{9,13},{10,... | collective-permute-start | bytes 786440 | tf_op jit(solution)/shard_map/ppermute | solution.py:326
  16.6 2.1 %collective-permute-start.5 = (bf16[1024,128]{1,0:T(8,128)(2,1)S(1)}, bf16[1024,128]{1,0:T(8,128)(2,1)S(1)}, u32[]{:S(2)}, u32[]{:S(2)}) collective-permute-start(bf16[1024,128]{1,0:T(8,128)(2,1)S(1)} %get-tuple-element.63), channel_id=1, source_target_pairs={{0,8},{1,9},{2,10},{3,11},{4,12},{5,13},{6,14},{7,15},{8,0},{9,1},... | collective-permute-start | bytes 786440 | tf_op jit(solution)/shard_map/ppermute | solution.py:326
  18.6 0.7 collective-permute-start.3
  19.5 1.8 %shard_map.64 = (bf16[1024,128]{1,0:T(8,128)(2,1)S(1)}, bf16[1024,128]{1,0:T(8,128)(2,1)}, bf16[1024,128]{1,0:T(8,128)(2,1)S(1)}, bf16[1024,128]{1,0:T(8,128)(2,...) custom-call(s32[16]{0:T(128)S(1)} %copy-done.3, ...), custom_call_target="tpu_custom_call" | custom-call | tf_op jit(solution)/shard_map/pallas_call | solution.py:42
  22.8 12.6 %collective-permute-done.refs_3_ = bf16[1024,128]{1,0:T(8,128)(2,1)S(1)} collective-permute-done((bf16[1024,128]{1,0:T(8,128)(2,1)S(1)}, bf16[1024,128]{1,0:T(8,128)(2,1)S(1)}, u32[]{:S(2)}, u32[]{:S(2)}) %collective-permute-start) | collective-permute-done | bytes 262176 | tf_op jit(solution)/shard_map/ppermute | solution.py:326
  35.4 2.5 %collective-permute-start.1 = (bf16[1024,128]{1,0:T(8,128)(2,1)S(1)}, bf16[1024,128]{1,0:T(8,128)(2,1)S(1)}, u32[]{:S(2)}, u32[]{:S(2)}) collective-permute-start(bf16[1024,128]{1,0:T(8,128)(2,1)S(1)} %get-tuple-element.51), channel_id=1, source_target_pairs={{0,3},{1,2},{2,1},{3,0},{4,7},{5,6},{6,5},{7,4},{8,11},{9,10},{10,... | collective-permute-start | bytes 786440 | tf_op jit(solution)/shard_map/ppermute | solution.py:326
  37.9 3.2 %collective-permute-done.4.refs_2_ = bf16[1024,128]{1,0:T(8,128)(2,1)S(1)} collective-permute-done((bf16[1024,128]{1,0:T(8,128)(2,1)S(1)}, bf16[1024,128]{1,0:T(8,128)(2,1)S(1)}, u32[]{:S(2)}, u32[]{:S(2)}) %collective-permute-start.4) | collective-permute-done | bytes 262176 | tf_op jit(solution)/shard_map/ppermute | solution.py:326
  41.1 3.1 %collective-permute-start.9 = (bf16[1024,128]{1,0:T(8,128)(2,1)S(1)}, bf16[1024,128]{1,0:T(8,128)(2,1)S(1)}, u32[]{:S(2)}, u32[]{:S(2)}) collective-permute-start(bf16[1024,128]{1,0:T(8,128)(2,1)S(1)} %get-tuple-element.77), channel_id=1, source_target_pairs={{0,6},{1,7},{2,4},{3,5},{4,2},{5,3},{6,0},{7,1},{8,14},{9,15},{10,... | collective-permute-start | bytes 786440 | tf_op jit(solution)/shard_map/ppermute | solution.py:326
  44.7 2.5 %collective-permute-done.6.refs_5_ = bf16[1024,128]{1,0:T(8,128)(2,1)S(1)} collective-permute-done((bf16[1024,128]{1,0:T(8,128)(2,1)S(1)}, bf16[1024,128]{1,0:T(8,128)(2,1)S(1)}, u32[]{:S(2)}, u32[]{:S(2)}) %collective-permute-start.6) | collective-permute-done | bytes 262176 | tf_op jit(solution)/shard_map/ppermute | solution.py:326
  47.2 0.7 copy-done.8
  47.9 3.6 %collective-permute-start.7 = (bf16[1024,128]{1,0:T(8,128)(2,1)}, bf16[1024,128]{1,0:T(8,128)(2,1)}, u32[]{:S(2)}, u32[]{:S(2)}) collective-permute-start(bf16[1024,128]{1,0:T(8,128)(2,1)} %get-tuple-element.74), channel_id=1, source_target_pairs={{0,11},{1,10},{2,9},{3,8},{4,15},{5,14},{6,13},{7,12},{8,3},{9,2},... | collective-permute-start | bytes 786440 | tf_op jit(solution)/shard_map/ppermute | solution.py:326
  52.3 1.2 collective-permute-start.2
  53.5 2.0 %collective-permute-done.9.refs_2_ = bf16[1024,128]{1,0:T(8,128)(2,1)S(1)} collective-permute-done((bf16[1024,128]{1,0:T(8,128)(2,1)S(1)}, bf16[1024,128]{1,0:T(8,128)(2,1)S(1)}, u32[]{:S(2)}, u32[]{:S(2)}) %collective-permute-start.9) | collective-permute-done | bytes 262176 | tf_op jit(solution)/shard_map/ppermute | solution.py:326
  56.2 1.7 %collective-permute-start.10 = (bf16[1024,128]{1,0:T(8,128)(2,1)S(1)}, bf16[1024,128]{1,0:T(8,128)(2,1)S(1)}, u32[]{:S(2)}, u32[]{:S(2)}) collective-permute-start(bf16[1024,128]{1,0:T(8,128)(2,1)S(1)} %get-tuple-element.78), channel_id=1, source_target_pairs={{0,12},{1,13},{2,14},{3,15},{4,8},{5,9},{6,10},{7,11},{8,4},{9,5},... | collective-permute-start | bytes 786440 | tf_op jit(solution)/shard_map/ppermute | solution.py:326
  57.9 16.8 %collective-permute-done.11.refs_4_ = bf16[1024,128]{1,0:T(8,128)(2,1)S(1)} collective-permute-done((bf16[1024,128]{1,0:T(8,128)(2,1)S(1)}, bf16[1024,128]{1,0:T(8,128)(2,1)S(1)}, u32[]{:S(2)}, u32[]{:S(2)}) %collective-permute-start.11) | collective-permute-done | bytes 262176 | tf_op jit(solution)/shard_map/ppermute | solution.py:326
  75.4 2.4 %collective-permute-start.12 = (bf16[1024,128]{1,0:T(8,128)(2,1)S(1)}, bf16[1024,128]{1,0:T(8,128)(2,1)S(1)}, u32[]{:S(2)}, u32[]{:S(2)}) collective-permute-start(bf16[1024,128]{1,0:T(8,128)(2,1)S(1)} %get-tuple-element.81), channel_id=1, source_target_pairs={{0,13},{1,12},{2,15},{3,14},{4,9},{5,8},{6,11},{7,10},{8,5},{9,4},... | collective-permute-start | bytes 786440 | tf_op jit(solution)/shard_map/ppermute | solution.py:326
  77.8 1.7 %shard_map.67 = (bf16[128,768]{1,0:T(8,128)(2,1)S(1)}, bf16[768,128]{1,0:T(8,128)(2,1)S(1)}, bf16[8,96,128]{2,1,0:T(8,128)(2,1)S(1)}) custom-call(s32[16]{0:T(128)S(1)} %copy-done.5, f32[48]{0:T(128)S(1)} %copy-done.6, bf16[16,144,128]{2,1,0:T(8,128)(2,1)S(1)} %all-to-all-done.matrix_ref), custom_call_target="tpu_custom_call" | custom-call | tf_op jit(solution)/shard_map/pallas_call | solution.py:145
  79.5 3.1 %collective-permute-start.14 = (bf16[1024,128]{1,0:T(8,128)(2,1)}, bf16[1024,128]{1,0:T(8,128)(2,1)S(1)}, u32[]{:S(2)}, u32[]{:S(2)}) collective-permute-start(bf16[1024,128]{1,0:T(8,128)(2,1)} %copy-done.7), channel_id=1, source_target_pairs={{0,7},{1,6},{2,5},{3,4},{4,3},{5,2},{6,1},{7,0},{8,15},{9,14},{10,... | collective-permute-start | bytes 786440 | tf_op jit(solution)/shard_map/ppermute | solution.py:326
  82.6 0.9 copy-done.9
  83.6 0.9 copy-done.11
  84.5 9.3 %shard_map.68.refs_9_ = bf16[128,128,128]{2,1,0:T(8,128)(2,1)S(1)} custom-call(bf16[1024,128]{1,0:T(8,128)(2,1)S(1)} %copy-done.11, bf16[1024,128]{1,0:T(8,128)(2,1)S(1)} %collective-permute-done.3.refs_1_, bf16[1024,128]{1,0:T(8,128)(2,1)S(1)} %collective-permute-done.4.refs_2_, bf16[1024,128]{1,0:T(8,128)(2,1)S(1)} %collective-permute-done.refs_3_, ...), custom_call_target="tpu_custom_call" | custom-call | flops 3623878656 | bytes 25165824 | tf_op jit(solution)/shard_map/pallas_call | solution.py:285
  93.8 3.5 %collective-permute-start.8 = (bf16[1024,128]{1,0:T(8,128)(2,1)S(1)}, bf16[1024,128]{1,0:T(8,128)(2,1)S(1)}, u32[]{:S(2)}, u32[]{:S(2)}) collective-permute-start(bf16[1024,128]{1,0:T(8,128)(2,1)S(1)} %get-tuple-element.75), channel_id=1, source_target_pairs={{0,15},{1,14},{2,13},{3,12},{4,11},{5,10},{6,9},{7,8},{8,7},{9,6},... | collective-permute-start | bytes 786440 | tf_op jit(solution)/shard_map/ppermute | solution.py:326
  97.4 10.8 %shard_map.69.refs_5_ = bf16[128,128,128]{2,1,0:T(8,128)(2,1)S(1)} custom-call(bf16[1024,128]{1,0:T(8,128)(2,1)} %collective-permute-done.13.refs_0_, bf16[1024,128]{1,0:T(8,128)(2,1)S(1)} %copy-done.13, bf16[1024,128]{1,0:T(8,128)(2,1)S(1)} %copy-done.15, bf16[1024,128]{1,0:T(8,128)(2,1)S(1)} %collective-permute-done.14.refs_3_, ...), custom_call_target="tpu_custom_call" | custom-call | flops 3623878656 | bytes 25165824 | tf_op jit(solution)/shard_map/pallas_call | solution.py:285
  108.1 6.2 %collective-permute-done.12.refs_1_ = bf16[1024,128]{1,0:T(8,128)(2,1)S(1)} collective-permute-done((bf16[1024,128]{1,0:T(8,128)(2,1)S(1)}, bf16[1024,128]{1,0:T(8,128)(2,1)S(1)}, u32[]{:S(2)}, u32[]{:S(2)}) %collective-permute-start.12) | collective-permute-done | bytes 262176 | tf_op jit(solution)/shard_map/ppermute | solution.py:326
  114.3 3.8 %shard_map.70.refs_5_ = bf16[128,128,128]{2,1,0:T(8,128)(2,1)S(1)} custom-call(bf16[1024,128]{1,0:T(8,128)(2,1)S(1)} %collective-permute-done.10.refs_0_, bf16[1024,128]{1,0:T(8,128)(2,1)S(1)} %collective-permute-done.12.refs_1_, bf16[128,768]{1,0:T(8,128)(2,1)S(1)} %get-tuple-element.70.refs_6_.refs_2_, ...), custom_call_target="tpu_custom_call" | custom-call | flops 1207959552 | bytes 25165824 | tf_op jit(solution)/shard_map/pallas_call | solution.py:285
  118.2 2.9 %collective-permute-done.8.refs_1_ = bf16[1024,128]{1,0:T(8,128)(2,1)S(1)} collective-permute-done((bf16[1024,128]{1,0:T(8,128)(2,1)S(1)}, bf16[1024,128]{1,0:T(8,128)(2,1)S(1)}, u32[]{:S(2)}, u32[]{:S(2)}) %collective-permute-start.8) | collective-permute-done | bytes 262176 | tf_op jit(solution)/shard_map/ppermute | solution.py:326
  121.1 6.3 %shard_map.71 = bf16[128,128,128]{2,1,0:T(8,128)(2,1)} custom-call(bf16[1024,128]{1,0:T(8,128)(2,1)S(1)} %collective-permute-done.2.refs_0_, bf16[1024,128]{1,0:T(8,128)(2,1)S(1)} %collective-permute-done.8.refs_1_, bf16[128,768]{1,0:T(8,128)(2,1)S(1)} %get-tuple-element.70.refs_6_.refs_2_, bf16[768,128]{1,0:T(8,128)(2,1)S(1)} %get-tuple-element.71.refs_7_.refs_3_, ...), custom_call_target="tpu_custom_call" | custom-call | flops 1207959552 | bytes 25165824 | tf_op jit(solution)/shard_map/pallas_call | solution.py:285
  (44 shorter events, 6.4 us)
Async XLA Ops:
  0.0 0.9 copy-start.1
  0.9 0.7 copy-start.2
  4.5 73.3 %all-to-all-start = ((bf16[16,144,128]{2,1,0:T(8,128)(2,1)}), bf16[16,144,128]{2,1,0:T(8,128)(2,1)S(1)}, u32[]{:S(2)}, u32[]{:S(2)}) async-start(bf16[16,144,128]{2,1,0:T(8,128)(2,1)} %shard_map.66), calls=%async_computation | async-start | bytes 1179648 | tf_op jit(solution)/shard_map/all_to_all | solution.py:331
  11.1 2.2 %copy-start = (bf16[16,1024,128]{2,1,0:T(8,128)(2,1)S(1)}, bf16[16,1024,128]{2,1,0:T(8,128)(2,1)}, u32[]{:S(2)}) copy-start(bf16[16,1024,128]{2,1,0:T(8,128)(2,1)} %source_ref.3) | copy-start | bytes 12582916
  13.9 63.9 %copy-start.5 = (s32[16]{0:T(128)S(1)}, s32[16]{0:T(128)}, u32[]{:S(2)}) copy-start(s32[16]{0:T(128)} %counts_ref.3) | copy-start | bytes 196
  13.9 63.9 %copy-start.6 = (f32[48]{0:T(128)S(1)}, f32[48]{0:T(128)}, u32[]{:S(2)}) copy-start(f32[48]{0:T(128)} %weights_ref.1) | copy-start | bytes 580
  14.8 20.6 %collective-permute-start = (bf16[1024,128]{1,0:T(8,128)(2,1)S(1)}, bf16[1024,128]{1,0:T(8,128)(2,1)S(1)}, u32[]{:S(2)}, u32[]{:S(2)}) collective-permute-start(bf16[1024,128]{1,0:T(8,128)(2,1)S(1)} %get-tuple-element.50), channel_id=1, source_target_pairs={{0,5},{1,4},{2,7},{3,6},{4,1},{5,0},{6,3},{7,2},{8,13},{9,12},{10,... | collective-permute-start | bytes 786440 | tf_op jit(solution)/shard_map/ppermute | solution.py:326
  14.9 26.2 %collective-permute-start.4 = (bf16[1024,128]{1,0:T(8,128)(2,1)S(1)}, bf16[1024,128]{1,0:T(8,128)(2,1)S(1)}, u32[]{:S(2)}, u32[]{:S(2)}) collective-permute-start(bf16[1024,128]{1,0:T(8,128)(2,1)S(1)} %get-tuple-element.59), channel_id=1, source_target_pairs={{0,4},{1,5},{2,6},{3,7},{4,0},{5,1},{6,2},{7,3},{8,12},{9,13},{10,... | collective-permute-start | bytes 786440 | tf_op jit(solution)/shard_map/ppermute | solution.py:326
  16.6 27.6 %collective-permute-start.5 = (bf16[1024,128]{1,0:T(8,128)(2,1)S(1)}, bf16[1024,128]{1,0:T(8,128)(2,1)S(1)}, u32[]{:S(2)}, u32[]{:S(2)}) collective-permute-start(bf16[1024,128]{1,0:T(8,128)(2,1)S(1)} %get-tuple-element.63), channel_id=1, source_target_pairs={{0,8},{1,9},{2,10},{3,11},{4,12},{5,13},{6,14},{7,15},{8,0},{9,1},... | collective-permute-start | bytes 786440 | tf_op jit(solution)/shard_map/ppermute | solution.py:326
  18.6 25.6 %collective-permute-start.3 = (bf16[1024,128]{1,0:T(8,128)(2,1)S(1)}, bf16[1024,128]{1,0:T(8,128)(2,1)S(1)}, u32[]{:S(2)}, u32[]{:S(2)}) collective-permute-start(bf16[1024,128]{1,0:T(8,128)(2,1)S(1)} %get-tuple-element.56), channel_id=1, source_target_pairs={{0,1},{1,0},{2,3},{3,2},{4,5},{5,4},{6,7},{7,6},{8,9},{9,8},{10,11... | collective-permute-start | bytes 786440 | tf_op jit(solution)/shard_map/ppermute | solution.py:326
  19.4 27.8 %collective-permute-start.6 = (bf16[1024,128]{1,0:T(8,128)(2,1)S(1)}, bf16[1024,128]{1,0:T(8,128)(2,1)S(1)}, u32[]{:S(2)}, u32[]{:S(2)}) collective-permute-start(bf16[1024,128]{1,0:T(8,128)(2,1)S(1)} %get-tuple-element.66), channel_id=1, source_target_pairs={{0,9},{1,8},{2,11},{3,10},{4,13},{5,12},{6,15},{7,14},{8,1},{9,0},... | collective-permute-start | bytes 786440 | tf_op jit(solution)/shard_map/ppermute | solution.py:326
  21.4 0.7 copy-start.7
  22.1 0.7 copy-start.10
  35.4 16.2 %collective-permute-start.1 = (bf16[1024,128]{1,0:T(8,128)(2,1)S(1)}, bf16[1024,128]{1,0:T(8,128)(2,1)S(1)}, u32[]{:S(2)}, u32[]{:S(2)}) collective-permute-start(bf16[1024,128]{1,0:T(8,128)(2,1)S(1)} %get-tuple-element.51), channel_id=1, source_target_pairs={{0,3},{1,2},{2,1},{3,0},{4,7},{5,6},{6,5},{7,4},{8,11},{9,10},{10,... | collective-permute-start | bytes 786440 | tf_op jit(solution)/shard_map/ppermute | solution.py:326
  41.1 14.4 %collective-permute-start.9 = (bf16[1024,128]{1,0:T(8,128)(2,1)S(1)}, bf16[1024,128]{1,0:T(8,128)(2,1)S(1)}, u32[]{:S(2)}, u32[]{:S(2)}) collective-permute-start(bf16[1024,128]{1,0:T(8,128)(2,1)S(1)} %get-tuple-element.77), channel_id=1, source_target_pairs={{0,6},{1,7},{2,4},{3,5},{4,2},{5,3},{6,0},{7,1},{8,14},{9,15},{10,... | collective-permute-start | bytes 786440 | tf_op jit(solution)/shard_map/ppermute | solution.py:326
  44.2 30.5 %collective-permute-start.11 = (bf16[1024,128]{1,0:T(8,128)(2,1)S(1)}, bf16[1024,128]{1,0:T(8,128)(2,1)S(1)}, u32[]{:S(2)}, u32[]{:S(2)}) collective-permute-start(bf16[1024,128]{1,0:T(8,128)(2,1)S(1)} %get-tuple-element.80), channel_id=1, source_target_pairs={{0,10},{1,11},{2,8},{3,9},{4,14},{5,15},{6,12},{7,13},{8,2},{9,3},... | collective-permute-start | bytes 786440 | tf_op jit(solution)/shard_map/ppermute | solution.py:326
  44.3 35.2 %collective-permute-start.13 = (bf16[1024,128]{1,0:T(8,128)(2,1)}, bf16[1024,128]{1,0:T(8,128)(2,1)}, u32[]{:S(2)}, u32[]{:S(2)}) collective-permute-start(bf16[1024,128]{1,0:T(8,128)(2,1)} %get-tuple-element.83), channel_id=1, source_target_pairs={{0,2},{1,3},{2,0},{3,1},{4,6},{5,7},{6,4},{7,5},{8,10},{9,11},{10,... | collective-permute-start | bytes 786440 | tf_op jit(solution)/shard_map/ppermute | solution.py:326
  47.2 0.7 copy-start.8
  47.9 45.9 %collective-permute-start.7 = (bf16[1024,128]{1,0:T(8,128)(2,1)}, bf16[1024,128]{1,0:T(8,128)(2,1)}, u32[]{:S(2)}, u32[]{:S(2)}) collective-permute-start(bf16[1024,128]{1,0:T(8,128)(2,1)} %get-tuple-element.74), channel_id=1, source_target_pairs={{0,11},{1,10},{2,9},{3,8},{4,15},{5,14},{6,13},{7,12},{8,3},{9,2},... | collective-permute-start | bytes 786440 | tf_op jit(solution)/shard_map/ppermute | solution.py:326
  51.6 0.7 copy-start.12
  52.3 65.9 %collective-permute-start.2 = (bf16[1024,128]{1,0:T(8,128)(2,1)S(1)}, bf16[1024,128]{1,0:T(8,128)(2,1)S(1)}, u32[]{:S(2)}, u32[]{:S(2)}) collective-permute-start(bf16[1024,128]{1,0:T(8,128)(2,1)S(1)} %get-tuple-element.52), channel_id=1, source_target_pairs={{0,14},{1,15},{2,12},{3,13},{4,10},{5,11},{6,8},{7,9},{8,6},{9,7},... | collective-permute-start | bytes 786440 | tf_op jit(solution)/shard_map/ppermute | solution.py:326
  55.5 0.7 copy-start.14
  56.2 51.9 %collective-permute-start.10 = (bf16[1024,128]{1,0:T(8,128)(2,1)S(1)}, bf16[1024,128]{1,0:T(8,128)(2,1)S(1)}, u32[]{:S(2)}, u32[]{:S(2)}) collective-permute-start(bf16[1024,128]{1,0:T(8,128)(2,1)S(1)} %get-tuple-element.78), channel_id=1, source_target_pairs={{0,12},{1,13},{2,14},{3,15},{4,8},{5,9},{6,10},{7,11},{8,4},{9,5},... | collective-permute-start | bytes 786440 | tf_op jit(solution)/shard_map/ppermute | solution.py:326
  74.7 0.7 copy-start.16
  75.4 38.9 %collective-permute-start.12 = (bf16[1024,128]{1,0:T(8,128)(2,1)S(1)}, bf16[1024,128]{1,0:T(8,128)(2,1)S(1)}, u32[]{:S(2)}, u32[]{:S(2)}) collective-permute-start(bf16[1024,128]{1,0:T(8,128)(2,1)S(1)} %get-tuple-element.81), channel_id=1, source_target_pairs={{0,13},{1,12},{2,15},{3,14},{4,9},{5,8},{6,11},{7,10},{8,5},{9,4},... | collective-permute-start | bytes 786440 | tf_op jit(solution)/shard_map/ppermute | solution.py:326
  79.5 17.8 %collective-permute-start.14 = (bf16[1024,128]{1,0:T(8,128)(2,1)}, bf16[1024,128]{1,0:T(8,128)(2,1)S(1)}, u32[]{:S(2)}, u32[]{:S(2)}) collective-permute-start(bf16[1024,128]{1,0:T(8,128)(2,1)} %copy-done.7), channel_id=1, source_target_pairs={{0,7},{1,6},{2,5},{3,4},{4,3},{5,2},{6,1},{7,0},{8,15},{9,14},{10,... | collective-permute-start | bytes 786440 | tf_op jit(solution)/shard_map/ppermute | solution.py:326
  82.6 0.9 copy-start.9
  83.6 0.9 copy-start.11
  84.5 12.8 %copy-start.13 = (bf16[1024,128]{1,0:T(8,128)(2,1)S(1)}, bf16[1024,128]{1,0:T(8,128)(2,1)}, u32[]{:S(2)}) copy-start(bf16[1024,128]{1,0:T(8,128)(2,1)} %copy-done.12) | copy-start | bytes 786436
  84.5 12.8 %copy-start.15 = (bf16[1024,128]{1,0:T(8,128)(2,1)S(1)}, bf16[1024,128]{1,0:T(8,128)(2,1)}, u32[]{:S(2)}) copy-start(bf16[1024,128]{1,0:T(8,128)(2,1)} %copy-done.14) | copy-start | bytes 786436
  84.5 12.8 %copy-start.17 = (bf16[1024,128]{1,0:T(8,128)(2,1)S(1)}, bf16[1024,128]{1,0:T(8,128)(2,1)}, u32[]{:S(2)}) copy-start(bf16[1024,128]{1,0:T(8,128)(2,1)} %copy-done.16) | copy-start | bytes 786436
  93.8 27.3 %collective-permute-start.8 = (bf16[1024,128]{1,0:T(8,128)(2,1)S(1)}, bf16[1024,128]{1,0:T(8,128)(2,1)S(1)}, u32[]{:S(2)}, u32[]{:S(2)}) collective-permute-start(bf16[1024,128]{1,0:T(8,128)(2,1)S(1)} %get-tuple-element.75), channel_id=1, source_target_pairs={{0,15},{1,14},{2,13},{3,12},{4,11},{5,10},{6,9},{7,8},{8,7},{9,6},... | collective-permute-start | bytes 786440 | tf_op jit(solution)/shard_map/ppermute | solution.py:326
  (2 other events, 1.3 us)

commit v5 on v3

--- a/solution.py
+++ b/solution.py
@@ -12,7 +12,7 @@
 UNIT_ROWS = 16
 B_BLOCK = 64
 ACC = jnp.bfloat16
-GROUPS = ((0, 2, 4), (1, 3, 5), (6,), (7,))
+GROUPS = ((0, 2), (1, 3, 4, 5), (6,), (7,))
 IN_FLIGHT = 5
 FAR_TURNS = (2, 4)
 SMALL_VMEM = 16 * 1024 * 1024

time: 128 us -> 124 us (0.969)
  starting transfers between devices: 32.9 us -> 30.5 us
    ppermute x15, starting transfers between devices: 26.3 us -> 23.9 us  [send(): lax.ppermute(piece, 'work', [(i, i ^ shift) for i in range(workers)])]
  transfers between devices with their start and end apart: 16 -> 16, of which waited for: 8 -> 9; matrix products, arithmetic and copies ran while one was open for 0% -> 0% of each run, Pallas kernels for 21% -> 21%
where the time goes in v5:
time: 124 us; the launch traced here: 123 us
  waiting for transfers between devices  46.7 us (38%)
  Pallas kernels  34.7 us (28%)
  starting transfers between devices  30.5 us (25%)
  local copies, waits for them, and re-layouts  11.2 us (9%)
    ppermute x15, waiting for transfers between devices, send(): lax.ppermute(piece, 'work', [(i, i ^ shift) for i in range(workers)])  46.7 us
    pallas_call x4, Pallas kernels, add_group(): pl.pallas_call(functools.partial(group_kernel, first, last, units, per_un...  28 us
    ppermute x15, starting transfers between devices, send(): lax.ppermute(piece, 'work', [(i, i ^ shift) for i in range(workers)])  23.9 us
    unnamed x38, local copies, waits for them, and re-layouts  11.2 us
    all_to_all x1, starting transfers between devices, per_device(): lax.all_to_all(matrices, 'work', split_axis=0, concat_axis=0, tiled=True)  6.61 us
    pallas_call x2, Pallas kernels, choose_pieces(): pl.pallas_call(functools.partial(pieces_kernel, shifts), in_specs=[pl.Blo...  2.75 us
  transfers between devices with their start and end apart: 16, of which 9 were waited for; matrix products, arithmetic and copies ran while one was open for 0% of the time, Pallas kernels for 21%

profile of v5, /device:TPU:11, one launch (start us, length us, event | category | flops | bytes accessed | tf_op | source)
XLA Modules:
  0.0 123.4 jit_solution(13594590908037454148)
XLA Ops:
  0.0 0.9 copy-done.1
  2.3 2.2 %shard_map.66 = bf16[16,144,128]{2,1,0:T(8,128)(2,1)} custom-call(s32[16]{0:T(128)S(1)} %copy-done.4, s32[3,48]{1,0:T(4,128)S(1)} %bitcast.2, bf16[96,1024]{1,0:T(8,128)(2,1)S(1)} %copy-done.1), custom_call_target="tpu_custom_call" | custom-call | tf_op jit(solution)/shard_map/pallas_call | solution.py:89
  4.5 6.6 %all-to-all-start = ((bf16[16,144,128]{2,1,0:T(8,128)(2,1)}), bf16[16,144,128]{2,1,0:T(8,128)(2,1)S(1)}, u32[]{:S(2)}, u32[]{:S(2)}) async-start(bf16[16,144,128]{2,1,0:T(8,128)(2,1)} %shard_map.66), calls=%async_computation | async-start | bytes 1179648 | tf_op jit(solution)/shard_map/all_to_all | solution.py:331
  11.1 2.2 %copy-done = bf16[16,1024,128]{2,1,0:T(8,128)(2,1)S(1)} copy-done((bf16[16,1024,128]{2,1,0:T(8,128)(2,1)S(1)}, bf16[16,1024,128]{2,1,0:T(8,128)(2,1)}, u32[]{:S(2)}) %copy-start) | copy-done | bytes 4194328
  13.9 0.9 shard_map.65
  15.3 1.4 %collective-permute-start.4 = (bf16[1024,128]{1,0:T(8,128)(2,1)S(1)}, bf16[1024,128]{1,0:T(8,128)(2,1)S(1)}, u32[]{:S(2)}, u32[]{:S(2)}) collective-permute-start(bf16[1024,128]{1,0:T(8,128)(2,1)S(1)} %get-tuple-element.57), channel_id=1, source_target_pairs={{0,4},{1,5},{2,6},{3,7},{4,0},{5,1},{6,2},{7,3},{8,12},{9,13},{10,... | collective-permute-start | bytes 786440 | tf_op jit(solution)/shard_map/ppermute | solution.py:326
  16.7 2.1 %collective-permute-start.10 = (bf16[1024,128]{1,0:T(8,128)(2,1)S(1)}, bf16[1024,128]{1,0:T(8,128)(2,1)S(1)}, u32[]{:S(2)}, u32[]{:S(2)}) collective-permute-start(bf16[1024,128]{1,0:T(8,128)(2,1)S(1)} %get-tuple-element.73), channel_id=1, source_target_pairs={{0,8},{1,9},{2,10},{3,11},{4,12},{5,13},{6,14},{7,15},{8,0},{9,1},... | collective-permute-start | bytes 786440 | tf_op jit(solution)/shard_map/ppermute | solution.py:326
  18.8 1.1 collective-permute-start.5
  19.9 1.9 %shard_map.64 = (bf16[1024,128]{1,0:T(8,128)(2,1)S(1)}, bf16[1024,128]{1,0:T(8,128)(2,1)S(1)}, bf16[1024,128]{1,0:T(8,128)(2,1)S(1)}, bf16[1024,128]{1,0:T(8,128...) custom-call(s32[16]{0:T(128)S(1)} %copy-done.3, ...), custom_call_target="tpu_custom_call" | custom-call | tf_op jit(solution)/shard_map/pallas_call | solution.py:42
  22.5 1.2 collective-permute-start.13
  23.7 11.7 %collective-permute-done.refs_3_ = bf16[1024,128]{1,0:T(8,128)(2,1)S(1)} collective-permute-done((bf16[1024,128]{1,0:T(8,128)(2,1)S(1)}, bf16[1024,128]{1,0:T(8,128)(2,1)S(1)}, u32[]{:S(2)}, u32[]{:S(2)}) %collective-permute-start) | collective-permute-done | bytes 262176 | tf_op jit(solution)/shard_map/ppermute | solution.py:326
  35.4 2.5 %collective-permute-start.1 = (bf16[1024,128]{1,0:T(8,128)(2,1)S(1)}, bf16[1024,128]{1,0:T(8,128)(2,1)S(1)}, u32[]{:S(2)}, u32[]{:S(2)}) collective-permute-start(bf16[1024,128]{1,0:T(8,128)(2,1)S(1)} %get-tuple-element.49), channel_id=1, source_target_pairs={{0,3},{1,2},{2,1},{3,0},{4,7},{5,6},{6,5},{7,4},{8,11},{9,10},{10,... | collective-permute-start | bytes 786440 | tf_op jit(solution)/shard_map/ppermute | solution.py:326
  37.9 3.2 %collective-permute-done.4.refs_2_ = bf16[1024,128]{1,0:T(8,128)(2,1)S(1)} collective-permute-done((bf16[1024,128]{1,0:T(8,128)(2,1)S(1)}, bf16[1024,128]{1,0:T(8,128)(2,1)S(1)}, u32[]{:S(2)}, u32[]{:S(2)}) %collective-permute-start.4) | collective-permute-done | bytes 262176 | tf_op jit(solution)/shard_map/ppermute | solution.py:326
  41.9 3.1 %collective-permute-start.8 = (bf16[1024,128]{1,0:T(8,128)(2,1)S(1)}, bf16[1024,128]{1,0:T(8,128)(2,1)S(1)}, u32[]{:S(2)}, u32[]{:S(2)}) collective-permute-start(bf16[1024,128]{1,0:T(8,128)(2,1)S(1)} %get-tuple-element.69), channel_id=1, source_target_pairs={{0,6},{1,7},{2,4},{3,5},{4,2},{5,3},{6,0},{7,1},{8,14},{9,15},{10,... | collective-permute-start | bytes 786440 | tf_op jit(solution)/shard_map/ppermute | solution.py:326
  45.0 1.9 %collective-permute-done.5.refs_5_ = bf16[1024,128]{1,0:T(8,128)(2,1)S(1)} collective-permute-done((bf16[1024,128]{1,0:T(8,128)(2,1)S(1)}, bf16[1024,128]{1,0:T(8,128)(2,1)S(1)}, u32[]{:S(2)}, u32[]{:S(2)}) %collective-permute-start.5) | collective-permute-done | bytes 262176 | tf_op jit(solution)/shard_map/ppermute | solution.py:326
  46.9 3.9 %collective-permute-start.6 = (bf16[1024,128]{1,0:T(8,128)(2,1)}, bf16[1024,128]{1,0:T(8,128)(2,1)}, u32[]{:S(2)}, u32[]{:S(2)}) collective-permute-start(bf16[1024,128]{1,0:T(8,128)(2,1)} %get-tuple-element.66), channel_id=1, source_target_pairs={{0,11},{1,10},{2,9},{3,8},{4,15},{5,14},{6,13},{7,12},{8,3},{9,2},... | collective-permute-start | bytes 786440 | tf_op jit(solution)/shard_map/ppermute | solution.py:326
  52.4 1.1 collective-permute-start.2
  53.5 2.7 %collective-permute-done.8.refs_2_ = bf16[1024,128]{1,0:T(8,128)(2,1)S(1)} collective-permute-done((bf16[1024,128]{1,0:T(8,128)(2,1)S(1)}, bf16[1024,128]{1,0:T(8,128)(2,1)S(1)}, u32[]{:S(2)}, u32[]{:S(2)}) %collective-permute-start.8) | collective-permute-done | bytes 262176 | tf_op jit(solution)/shard_map/ppermute | solution.py:326
  57.8 5.5 %collective-permute-done.11.refs_6_ = bf16[1024,128]{1,0:T(8,128)(2,1)S(1)} collective-permute-done((bf16[1024,128]{1,0:T(8,128)(2,1)S(1)}, bf16[1024,128]{1,0:T(8,128)(2,1)S(1)}, u32[]{:S(2)}, u32[]{:S(2)}) %collective-permute-start.11) | collective-permute-done | bytes 262176 | tf_op jit(solution)/shard_map/ppermute | solution.py:326
  64.0 2.5 %collective-permute-start.12 = (bf16[1024,128]{1,0:T(8,128)(2,1)S(1)}, bf16[1024,128]{1,0:T(8,128)(2,1)S(1)}, u32[]{:S(2)}, u32[]{:S(2)}) collective-permute-start(bf16[1024,128]{1,0:T(8,128)(2,1)S(1)} %get-tuple-element.75), channel_id=1, source_target_pairs={{0,13},{1,12},{2,15},{3,14},{4,9},{5,8},{6,11},{7,10},{8,5},{9,4},... | collective-permute-start | bytes 786440 | tf_op jit(solution)/shard_map/ppermute | solution.py:326
  66.5 1.7 %shard_map.67 = (bf16[128,768]{1,0:T(8,128)(2,1)S(1)}, bf16[768,128]{1,0:T(8,128)(2,1)S(1)}, bf16[8,96,128]{2,1,0:T(8,128)(2,1)S(1)}) custom-call(s32[16]{0:T(128)S(1)} %copy-done.5, f32[48]{0:T(128)S(1)} %copy-done.6, bf16[16,144,128]{2,1,0:T(8,128)(2,1)S(1)} %all-to-all-done.matrix_ref), custom_call_target="tpu_custom_call" | custom-call | tf_op jit(solution)/shard_map/pallas_call | solution.py:145
  68.3 0.9 copy-done.8
  69.2 0.9 copy-done.12
  70.2 5.8 %shard_map.68.refs_11_ = bf16[128,128,128]{2,1,0:T(8,128)(2,1)S(1)} custom-call(bf16[1024,128]{1,0:T(8,128)(2,1)S(1)} %copy-done.12, bf16[1024,128]{1,0:T(8,128)(2,1)S(1)} %collective-permute-done.3.refs_1_, bf16[1024,128]{1,0:T(8,128)(2,1)S(1)} %copy-done.8, bf16[1024,128]{1,0:T(8,128)(2,1)S(1)} %collective-permute-done.refs_3_, ...), custom_call_target="tpu_custom_call" | custom-call | flops 2415919104 | bytes 25165824 | tf_op jit(solution)/shard_map/pallas_call | solution.py:285
  76.0 9.9 %collective-permute-done.6.refs_7_ = bf16[1024,128]{1,0:T(8,128)(2,1)} collective-permute-done((bf16[1024,128]{1,0:T(8,128)(2,1)}, bf16[1024,128]{1,0:T(8,128)(2,1)}, u32[]{:S(2)}, u32[]{:S(2)}) %collective-permute-start.6) | collective-permute-done | bytes 262176 | tf_op jit(solution)/shard_map/ppermute | solution.py:326
  85.9 3.5 %collective-permute-start.7 = (bf16[1024,128]{1,0:T(8,128)(2,1)S(1)}, bf16[1024,128]{1,0:T(8,128)(2,1)S(1)}, u32[]{:S(2)}, u32[]{:S(2)}) collective-permute-start(bf16[1024,128]{1,0:T(8,128)(2,1)S(1)} %get-tuple-element.67), channel_id=1, source_target_pairs={{0,15},{1,14},{2,13},{3,12},{4,11},{5,10},{6,9},{7,8},{8,7},{9,6},... | collective-permute-start | bytes 786440 | tf_op jit(solution)/shard_map/ppermute | solution.py:326
  89.4 12.2 %shard_map.69.refs_5_ = bf16[128,128,128]{2,1,0:T(8,128)(2,1)S(1)} custom-call(bf16[1024,128]{1,0:T(8,128)(2,1)S(1)} %copy-done.10, bf16[1024,128]{1,0:T(8,128)(2,1)S(1)} %copy-done.14, bf16[1024,128]{1,0:T(8,128)(2,1)S(1)} %copy-done.16, bf16[1024,128]{1,0:T(8,128)(2,1)} %collective-permute-done.14.refs_3_, ...), custom_call_target="tpu_custom_call" | custom-call | flops 4831838208 | bytes 25165824 | tf_op jit(solution)/shard_map/pallas_call | solution.py:285
  101.6 3.1 %collective-permute-done.9.refs_0_ = bf16[1024,128]{1,0:T(8,128)(2,1)S(1)} collective-permute-done((bf16[1024,128]{1,0:T(8,128)(2,1)S(1)}, bf16[1024,128]{1,0:T(8,128)(2,1)S(1)}, u32[]{:S(2)}, u32[]{:S(2)}) %collective-permute-start.9) | collective-permute-done | bytes 262176 | tf_op jit(solution)/shard_map/ppermute | solution.py:326
  104.7 6.3 %collective-permute-done.12.refs_1_ = bf16[1024,128]{1,0:T(8,128)(2,1)S(1)} collective-permute-done((bf16[1024,128]{1,0:T(8,128)(2,1)S(1)}, bf16[1024,128]{1,0:T(8,128)(2,1)S(1)}, u32[]{:S(2)}, u32[]{:S(2)}) %collective-permute-start.12) | collective-permute-done | bytes 262176 | tf_op jit(solution)/shard_map/ppermute | solution.py:326
  110.9 3.8 %shard_map.70.refs_5_ = bf16[128,128,128]{2,1,0:T(8,128)(2,1)S(1)} custom-call(bf16[1024,128]{1,0:T(8,128)(2,1)S(1)} %collective-permute-done.9.refs_0_, bf16[1024,128]{1,0:T(8,128)(2,1)S(1)} %collective-permute-done.12.refs_1_, bf16[128,768]{1,0:T(8,128)(2,1)S(1)} %get-tuple-element.60.refs_4_.refs_8_.refs_2_, ...), custom_call_target="tpu_custom_call" | custom-call | flops 1207959552 | bytes 25165824 | tf_op jit(solution)/shard_map/pallas_call | solution.py:285
  114.8 2.3 %collective-permute-done.7.refs_1_ = bf16[1024,128]{1,0:T(8,128)(2,1)S(1)} collective-permute-done((bf16[1024,128]{1,0:T(8,128)(2,1)S(1)}, bf16[1024,128]{1,0:T(8,128)(2,1)S(1)}, u32[]{:S(2)}, u32[]{:S(2)}) %collective-permute-start.7) | collective-permute-done | bytes 262176 | tf_op jit(solution)/shard_map/ppermute | solution.py:326
  117.0 6.2 %shard_map.71 = bf16[128,128,128]{2,1,0:T(8,128)(2,1)} custom-call(bf16[1024,128]{1,0:T(8,128)(2,1)S(1)} %collective-permute-done.2.refs_0_, bf16[1024,128]{1,0:T(8,128)(2,1)S(1)} %collective-permute-done.7.refs_1_, bf16[128,768]{1,0:T(8,128)(2,1)S(1)} %get-tuple-element.60.refs_4_.refs_8_.refs_2_, ...), custom_call_target="tpu_custom_call" | custom-call | flops 1207959552 | bytes 25165824 | tf_op jit(solution)/shard_map/pallas_call | solution.py:285
  (46 shorter events, 7.8 us)
Async XLA Ops:
  0.0 0.9 copy-start.1
  4.5 62.1 %all-to-all-start = ((bf16[16,144,128]{2,1,0:T(8,128)(2,1)}), bf16[16,144,128]{2,1,0:T(8,128)(2,1)S(1)}, u32[]{:S(2)}, u32[]{:S(2)}) async-start(bf16[16,144,128]{2,1,0:T(8,128)(2,1)} %shard_map.66), calls=%async_computation | async-start | bytes 1179648 | tf_op jit(solution)/shard_map/all_to_all | solution.py:331
  11.1 2.2 %copy-start = (bf16[16,1024,128]{2,1,0:T(8,128)(2,1)S(1)}, bf16[16,1024,128]{2,1,0:T(8,128)(2,1)}, u32[]{:S(2)}) copy-start(bf16[16,1024,128]{2,1,0:T(8,128)(2,1)} %source_ref.3) | copy-start | bytes 12582916
  13.9 52.6 %copy-start.5 = (s32[16]{0:T(128)S(1)}, s32[16]{0:T(128)}, u32[]{:S(2)}) copy-start(s32[16]{0:T(128)} %counts_ref.3) | copy-start | bytes 196
  13.9 52.6 %copy-start.6 = (f32[48]{0:T(128)S(1)}, f32[48]{0:T(128)}, u32[]{:S(2)}) copy-start(f32[48]{0:T(128)} %weights_ref.1) | copy-start | bytes 580
  14.8 7.7 %collective-permute-start.3 = (bf16[1024,128]{1,0:T(8,128)(2,1)S(1)}, bf16[1024,128]{1,0:T(8,128)(2,1)S(1)}, u32[]{:S(2)}, u32[]{:S(2)}) collective-permute-start(bf16[1024,128]{1,0:T(8,128)(2,1)S(1)} %get-tuple-element.54), channel_id=1, source_target_pairs={{0,1},{1,0},{2,3},{3,2},{4,5},{5,4},{6,7},{7,6},{8,9},{9,8},{10,11... | collective-permute-start | bytes 786440 | tf_op jit(solution)/shard_map/ppermute | solution.py:326
  15.2 20.2 %collective-permute-start = (bf16[1024,128]{1,0:T(8,128)(2,1)S(1)}, bf16[1024,128]{1,0:T(8,128)(2,1)S(1)}, u32[]{:S(2)}, u32[]{:S(2)}) collective-permute-start(bf16[1024,128]{1,0:T(8,128)(2,1)S(1)} %get-tuple-element.48), channel_id=1, source_target_pairs={{0,5},{1,4},{2,7},{3,6},{4,1},{5,0},{6,3},{7,2},{8,13},{9,12},{10,... | collective-permute-start | bytes 786440 | tf_op jit(solution)/shard_map/ppermute | solution.py:326
  15.3 25.8 %collective-permute-start.4 = (bf16[1024,128]{1,0:T(8,128)(2,1)S(1)}, bf16[1024,128]{1,0:T(8,128)(2,1)S(1)}, u32[]{:S(2)}, u32[]{:S(2)}) collective-permute-start(bf16[1024,128]{1,0:T(8,128)(2,1)S(1)} %get-tuple-element.57), channel_id=1, source_target_pairs={{0,4},{1,5},{2,6},{3,7},{4,0},{5,1},{6,2},{7,3},{8,12},{9,13},{10,... | collective-permute-start | bytes 786440 | tf_op jit(solution)/shard_map/ppermute | solution.py:326
  16.7 28.2 %collective-permute-start.10 = (bf16[1024,128]{1,0:T(8,128)(2,1)S(1)}, bf16[1024,128]{1,0:T(8,128)(2,1)S(1)}, u32[]{:S(2)}, u32[]{:S(2)}) collective-permute-start(bf16[1024,128]{1,0:T(8,128)(2,1)S(1)} %get-tuple-element.73), channel_id=1, source_target_pairs={{0,8},{1,9},{2,10},{3,11},{4,12},{5,13},{6,14},{7,15},{8,0},{9,1},... | collective-permute-start | bytes 786440 | tf_op jit(solution)/shard_map/ppermute | solution.py:326
  18.8 28.1 %collective-permute-start.5 = (bf16[1024,128]{1,0:T(8,128)(2,1)S(1)}, bf16[1024,128]{1,0:T(8,128)(2,1)S(1)}, u32[]{:S(2)}, u32[]{:S(2)}) collective-permute-start(bf16[1024,128]{1,0:T(8,128)(2,1)S(1)} %get-tuple-element.65), channel_id=1, source_target_pairs={{0,9},{1,8},{2,11},{3,10},{4,13},{5,12},{6,15},{7,14},{8,1},{9,0},... | collective-permute-start | bytes 786440 | tf_op jit(solution)/shard_map/ppermute | solution.py:326
  21.8 0.7 copy-start.11
  22.5 28.4 %collective-permute-start.13 = (bf16[1024,128]{1,0:T(8,128)(2,1)S(1)}, bf16[1024,128]{1,0:T(8,128)(2,1)S(1)}, u32[]{:S(2)}, u32[]{:S(2)}) collective-permute-start(bf16[1024,128]{1,0:T(8,128)(2,1)S(1)} %get-tuple-element.77), channel_id=1, source_target_pairs={{0,2},{1,3},{2,0},{3,1},{4,6},{5,7},{6,4},{7,5},{8,10},{9,11},{10,... | collective-permute-start | bytes 786440 | tf_op jit(solution)/shard_map/ppermute | solution.py:326
  35.4 16.3 %collective-permute-start.1 = (bf16[1024,128]{1,0:T(8,128)(2,1)S(1)}, bf16[1024,128]{1,0:T(8,128)(2,1)S(1)}, u32[]{:S(2)}, u32[]{:S(2)}) collective-permute-start(bf16[1024,128]{1,0:T(8,128)(2,1)S(1)} %get-tuple-element.49), channel_id=1, source_target_pairs={{0,3},{1,2},{2,1},{3,0},{4,7},{5,6},{6,5},{7,4},{8,11},{9,10},{10,... | collective-permute-start | bytes 786440 | tf_op jit(solution)/shard_map/ppermute | solution.py:326
  41.2 0.7 copy-start.7
  41.9 14.3 %collective-permute-start.8 = (bf16[1024,128]{1,0:T(8,128)(2,1)S(1)}, bf16[1024,128]{1,0:T(8,128)(2,1)S(1)}, u32[]{:S(2)}, u32[]{:S(2)}) collective-permute-start(bf16[1024,128]{1,0:T(8,128)(2,1)S(1)} %get-tuple-element.69), channel_id=1, source_target_pairs={{0,6},{1,7},{2,4},{3,5},{4,2},{5,3},{6,0},{7,1},{8,14},{9,15},{10,... | collective-permute-start | bytes 786440 | tf_op jit(solution)/shard_map/ppermute | solution.py:326
  44.9 18.4 %collective-permute-start.11 = (bf16[1024,128]{1,0:T(8,128)(2,1)S(1)}, bf16[1024,128]{1,0:T(8,128)(2,1)S(1)}, u32[]{:S(2)}, u32[]{:S(2)}) collective-permute-start(bf16[1024,128]{1,0:T(8,128)(2,1)S(1)} %get-tuple-element.74), channel_id=1, source_target_pairs={{0,10},{1,11},{2,8},{3,9},{4,14},{5,15},{6,12},{7,13},{8,2},{9,3},... | collective-permute-start | bytes 786440 | tf_op jit(solution)/shard_map/ppermute | solution.py:326
  46.9 39.0 %collective-permute-start.6 = (bf16[1024,128]{1,0:T(8,128)(2,1)}, bf16[1024,128]{1,0:T(8,128)(2,1)}, u32[]{:S(2)}, u32[]{:S(2)}) collective-permute-start(bf16[1024,128]{1,0:T(8,128)(2,1)} %get-tuple-element.66), channel_id=1, source_target_pairs={{0,11},{1,10},{2,9},{3,8},{4,15},{5,14},{6,13},{7,12},{8,3},{9,2},... | collective-permute-start | bytes 786440 | tf_op jit(solution)/shard_map/ppermute | solution.py:326
  50.9 0.7 copy-start.9
  51.6 37.8 %collective-permute-start.14 = (bf16[1024,128]{1,0:T(8,128)(2,1)}, bf16[1024,128]{1,0:T(8,128)(2,1)}, u32[]{:S(2)}, u32[]{:S(2)}) collective-permute-start(bf16[1024,128]{1,0:T(8,128)(2,1)} %get-tuple-element.81), channel_id=1, source_target_pairs={{0,7},{1,6},{2,5},{3,4},{4,3},{5,2},{6,1},{7,0},{8,15},{9,14},{10,... | collective-permute-start | bytes 786440 | tf_op jit(solution)/shard_map/ppermute | solution.py:326
  51.7 0.7 copy-start.13
  52.4 62.4 %collective-permute-start.2 = (bf16[1024,128]{1,0:T(8,128)(2,1)S(1)}, bf16[1024,128]{1,0:T(8,128)(2,1)S(1)}, u32[]{:S(2)}, u32[]{:S(2)}) collective-permute-start(bf16[1024,128]{1,0:T(8,128)(2,1)S(1)} %get-tuple-element.50), channel_id=1, source_target_pairs={{0,14},{1,15},{2,12},{3,13},{4,10},{5,11},{6,8},{7,9},{8,6},{9,7},... | collective-permute-start | bytes 786440 | tf_op jit(solution)/shard_map/ppermute | solution.py:326
  56.2 0.7 copy-start.15
  56.9 47.7 %collective-permute-start.9 = (bf16[1024,128]{1,0:T(8,128)(2,1)S(1)}, bf16[1024,128]{1,0:T(8,128)(2,1)S(1)}, u32[]{:S(2)}, u32[]{:S(2)}) collective-permute-start(bf16[1024,128]{1,0:T(8,128)(2,1)S(1)} %get-tuple-element.70), channel_id=1, source_target_pairs={{0,12},{1,13},{2,14},{3,15},{4,8},{5,9},{6,10},{7,11},{8,4},{9,5},... | collective-permute-start | bytes 786440 | tf_op jit(solution)/shard_map/ppermute | solution.py:326
  63.3 0.7 copy-start.17
  64.0 46.9 %collective-permute-start.12 = (bf16[1024,128]{1,0:T(8,128)(2,1)S(1)}, bf16[1024,128]{1,0:T(8,128)(2,1)S(1)}, u32[]{:S(2)}, u32[]{:S(2)}) collective-permute-start(bf16[1024,128]{1,0:T(8,128)(2,1)S(1)} %get-tuple-element.75), channel_id=1, source_target_pairs={{0,13},{1,12},{2,15},{3,14},{4,9},{5,8},{6,11},{7,10},{8,5},{9,4},... | collective-permute-start | bytes 786440 | tf_op jit(solution)/shard_map/ppermute | solution.py:326
  68.2 1.0 copy-start.8
  69.2 0.9 copy-start.12
  70.1 19.2 %copy-start.10 = (bf16[1024,128]{1,0:T(8,128)(2,1)S(1)}, bf16[1024,128]{1,0:T(8,128)(2,1)}, u32[]{:S(2)}) copy-start(bf16[1024,128]{1,0:T(8,128)(2,1)} %copy-done.9) | copy-start | bytes 786436
  70.1 19.2 %copy-start.14 = (bf16[1024,128]{1,0:T(8,128)(2,1)S(1)}, bf16[1024,128]{1,0:T(8,128)(2,1)}, u32[]{:S(2)}) copy-start(bf16[1024,128]{1,0:T(8,128)(2,1)} %copy-done.13) | copy-start | bytes 786436
  70.1 19.2 %copy-start.16 = (bf16[1024,128]{1,0:T(8,128)(2,1)S(1)}, bf16[1024,128]{1,0:T(8,128)(2,1)}, u32[]{:S(2)}) copy-start(bf16[1024,128]{1,0:T(8,128)(2,1)} %copy-done.15) | copy-start | bytes 786436
  70.2 19.2 %copy-start.18 = (bf16[1024,128]{1,0:T(8,128)(2,1)S(1)}, bf16[1024,128]{1,0:T(8,128)(2,1)}, u32[]{:S(2)}) copy-start(bf16[1024,128]{1,0:T(8,128)(2,1)} %copy-done.17) | copy-start | bytes 786436
  85.9 31.1 %collective-permute-start.7 = (bf16[1024,128]{1,0:T(8,128)(2,1)S(1)}, bf16[1024,128]{1,0:T(8,128)(2,1)S(1)}, u32[]{:S(2)}, u32[]{:S(2)}) collective-permute-start(bf16[1024,128]{1,0:T(8,128)(2,1)S(1)} %get-tuple-element.67), channel_id=1, source_target_pairs={{0,15},{1,14},{2,13},{3,12},{4,11},{5,10},{6,9},{7,8},{8,7},{9,6},... | collective-permute-start | bytes 786440 | tf_op jit(solution)/shard_map/ppermute | solution.py:326
  (3 other events, 2.0 us)
